TPU v7x, 128 devices: a whole 4x4x4 slice. The times are simulated.
128 devices in a mesh: dp: 4 (over x), expert: 32 (over y, z, core).
Axes of the slice: x: 4, y: 4, z: 4, core: 2. Of those that a mesh axis runs over, the one named last changes fastest.
Arguments:
- tokens: bfloat16 [16384, 7168], P(('dp', 'expert')), may hold values from -6 to 6
- grad_out: bfloat16 [16384, 7168], P(('dp', 'expert')), may hold values from -1.5 to 1.5
- expert_ids: int32 [16384, 8], P(('dp', 'expert')), may hold values from 0 to 255, as said below
- gate_weights: float32 [16384, 8], P(('dp', 'expert')), may hold values from 0.2 to 1
- w_gate: bfloat16 [7168, 12288], P(None, 'expert'), may hold values from -0.0625 to 0.0625
- w_up: bfloat16 [7168, 12288], P(None, 'expert'), may hold values from -0.0625 to 0.0625
- w_down: bfloat16 [12288, 7168], P('expert'), may hold values from -0.15625 to 0.15625
Outputs:
- grad_tokens: bfloat16 [16384, 7168], P(('dp', 'expert'))
- grad_gate: bfloat16 [7168, 12288], P('dp', 'expert')
- grad_up: bfloat16 [7168, 12288], P('dp', 'expert')
- grad_down: bfloat16 [12288, 7168], P('expert', 'dp')
Inputs may be any that keep to these rules, and one draw needn't show every extreme that they name: `expert_ids`: the 8 ids of a token are distinct. Experts 0 to 7 are the experts in flight; no more than 8 tokens of one block of 128 choose any one of them, and in every draw one expert in flight is chosen by exactly 8 tokens of every block.
All inputs are finite; a program needn't handle non-finite values.
Results may differ from a plain program's by a relative error of at most 0.015.
Values may be sent and summed in bfloat16 or wider, within the bound.
A program may use at most 192 MiB of HBM per device.

v0:
```python
import jax
import jax.numpy as jnp
from jax import lax
from jax.sharding import PartitionSpec as P

SPLIT = 4
CAP = 8


def expert_terms(rows_in, rows_grad, gate_cols, up_cols, down_rows):
    gate_pre = jnp.dot(rows_in, gate_cols, preferred_element_type=jnp.float32)
    up_pre = jnp.dot(rows_in, up_cols, preferred_element_type=jnp.float32)
    sig = jax.nn.sigmoid(gate_pre)
    act = gate_pre * sig
    hidden = (act * up_pre).astype(jnp.bfloat16)
    d_hidden = lax.dot_general(
        rows_grad, down_rows, (((1,), (1,)), ((), ())), preferred_element_type=jnp.float32
    )
    d_gate = (d_hidden * up_pre * sig * (1.0 + gate_pre * (1.0 - sig))).astype(jnp.bfloat16)
    d_up = (d_hidden * act).astype(jnp.bfloat16)
    contract_cols = (((1,), (1,)), ((), ()))
    back = lax.dot_general(d_gate, gate_cols, contract_cols, preferred_element_type=jnp.float32)
    back = back + lax.dot_general(d_up, up_cols, contract_cols, preferred_element_type=jnp.float32)
    return (back, d_gate, d_up, hidden)


def weight_terms(rows_in, rows_grad, d_gate, d_up, hidden):
    contract_rows = (((0,), (0,)), ((), ()))
    g_gate = lax.dot_general(rows_in, d_gate, contract_rows, preferred_element_type=jnp.float32)
    g_up = lax.dot_general(rows_in, d_up, contract_rows, preferred_element_type=jnp.float32)
    g_down = lax.dot_general(hidden, rows_grad, contract_rows, preferred_element_type=jnp.float32)
    return (g_gate, g_up, g_down)


def body(tokens, grad_out, expert_ids, gate_weights, w_gate, w_up, w_down):
    peer_count = lax.axis_size("expert")
    experts = peer_count // SPLIT
    width = tokens.shape[1]
    chosen = expert_ids[None, :, :] == jnp.arange(experts, dtype=jnp.int32)[:, None, None]
    member = jnp.sum(chosen.astype(jnp.int32), axis=2)
    weight = jnp.sum(jnp.where(chosen, gate_weights[None, :, :], jnp.float32(0.0)), axis=2)
    position = jnp.cumsum(member, axis=1) - 1
    slot_mask = (member[..., None] == 1) & (position[..., None] == jnp.arange(CAP, dtype=jnp.int32))
    picker = slot_mask.astype(jnp.bfloat16)
    slot_inputs = jnp.einsum(
        "etc,td->ecd", picker, tokens, preferred_element_type=jnp.float32
    ).astype(jnp.bfloat16)
    raw_grads = jnp.einsum("etc,td->ecd", picker, grad_out, preferred_element_type=jnp.float32)
    slot_gate = jnp.sum(slot_mask.astype(jnp.float32) * weight[..., None], axis=1)
    slot_grads = (slot_gate[..., None] * raw_grads).astype(jnp.bfloat16)
    send_in = jnp.broadcast_to(slot_inputs[:, None], (experts, SPLIT, CAP, width)).reshape(
        peer_count, CAP, width
    )
    send_grad = jnp.broadcast_to(slot_grads[:, None], (experts, SPLIT, CAP, width)).reshape(
        peer_count, CAP, width
    )
    got_in, got_grad = (
        lax.all_to_all(send_in, "expert", split_axis=0, concat_axis=0, tiled=True),
        lax.all_to_all(send_grad, "expert", split_axis=0, concat_axis=0, tiled=True),
    )
    rows_in = got_in.reshape(peer_count * CAP, width)
    rows_grad = got_grad.reshape(peer_count * CAP, width)
    back, d_gate, d_up, hidden = expert_terms(rows_in, rows_grad, w_gate, w_up, w_down)
    parts = lax.all_to_all(
        back.reshape(peer_count, CAP, width).astype(jnp.bfloat16),
        "expert",
        split_axis=0,
        concat_axis=0,
        tiled=True,
    ).astype(jnp.float32)
    slot_back = jnp.sum(parts.reshape(experts, SPLIT, CAP, width), axis=1).astype(jnp.bfloat16)
    grad_tokens = jnp.einsum(
        "etc,ecd->td", picker, slot_back, preferred_element_type=jnp.float32
    ).astype(jnp.bfloat16)
    g_gate, g_up, g_down = weight_terms(rows_in, rows_grad, d_gate, d_up, hidden)
    sum_gate, sum_up, sum_down = (
        lax.psum_scatter(g_gate.astype(jnp.bfloat16), "dp", scatter_dimension=0, tiled=True).astype(
            jnp.float32
        ),
        lax.psum_scatter(g_up.astype(jnp.bfloat16), "dp", scatter_dimension=0, tiled=True).astype(
            jnp.float32
        ),
        lax.psum_scatter(g_down.astype(jnp.bfloat16), "dp", scatter_dimension=1, tiled=True).astype(
            jnp.float32
        ),
    )
    return (
        grad_tokens,
        sum_gate.astype(jnp.bfloat16),
        sum_up.astype(jnp.bfloat16),
        sum_down.astype(jnp.bfloat16),
    )


def solution(mesh):
    in_specs = (
        P(("dp", "expert"), None),
        P(("dp", "expert"), None),
        P(("dp", "expert"), None),
        P(("dp", "expert"), None),
        P(None, "expert"),
        P(None, "expert"),
        P("expert", None),
    )
    out_specs = (P(("dp", "expert"), None), P("dp", "expert"), P("dp", "expert"), P("expert", "dp"))
    return jax.shard_map(body, mesh=mesh, in_specs=in_specs, out_specs=out_specs, check_vma=False)
```

profile of v0, /device:TPU:1, one launch (start us, length us, event | category | flops | bytes accessed | tf_op | source)
XLA Modules:
  0.0 313.4 jit_solution(1040459254939859565)
XLA Ops:
  7.2 0.8 convert_reduce_fusion
  8.0 0.3 reduce_window_sum.11
  8.3 0.4 copy-done
  8.7 0.4 convolution_convert_fusion.3
  9.1 2.2 broadcast_in_dim.19
  11.3 9.8 %all-to-all-start.1 = ((bf16[32,8,7168]{2,1,0:T(8,128)(2,1)}), bf16[32,8,7168]{2,1,0:T(8,128)(2,1)}, u32[]{:S(2)}, u32[]{:S(2)}) async-start(bf16[32,8,7168]{2,1,0:T(8,128)(2,1)} %bitcast.41), calls=%async_computation.1 | async-start | bytes 7340032 | tf_op jit(solution)/shard_map/all_to_all | solution.py:58
  21.2 0.1 select_reduce_fusion
  21.2 0.1 copy.13
  21.3 1.9 fusion.3
  23.2 43.9 %all-to-all-done.1 = bf16[32,8,7168]{2,1,0:T(8,128)(2,1)} async-done(((bf16[32,8,7168]{2,1,0:T(8,128)(2,1)}), bf16[32,8,7168]{2,1,0:T(8,128)(2,1)}, u32[]{:S(2)}, u32[]{:S(2)}) %all-to-all-start.1) | async-done | bytes 3670048 | tf_op jit(solution)/shard_map/all_to_all | solution.py:58
  67.1 2.2 broadcast_in_dim.18
  69.4 6.8 %all-to-all-start = ((bf16[32,8,7168]{2,1,0:T(8,128)(2,1)}), bf16[32,8,7168]{2,1,0:T(8,128)(2,1)}, u32[]{:S(2)}, u32[]{:S(2)}) async-start(bf16[32,8,7168]{2,1,0:T(8,128)(2,1)} %bitcast.42), calls=%async_computation | async-start | bytes 7340032 | tf_op jit(solution)/shard_map/all_to_all | solution.py:59
  76.2 0.0 reduce-scatter.8.cloned.1.call-start
  76.2 5.8 %fusion.6 = f32[256,384]{1,0:T(8,128)S(1)} fusion(bf16[7168,384]{1,0:T(8,128)(2,1)} %param.11, bf16[32,8,7168]{2,1,0:T(8,128)(2,1)} %all-to-all-done.1), kind=kOutput, calls=%fused_computation.14 | convolution fusion | flops 1409286144 | bytes 9568256 | tf_op jit(solution)/shard_map/dot_general | solution.py:11
  82.0 5.8 %fusion.8 = f32[256,384]{1,0:T(8,128)S(1)} fusion(bf16[7168,384]{1,0:T(8,128)(2,1)} %param.12, bf16[32,8,7168]{2,1,0:T(8,128)(2,1)} %all-to-all-done.1), kind=kOutput, calls=%fused_computation.16 | convolution fusion | flops 1409286144 | bytes 9568256 | tf_op jit(solution)/shard_map/dot_general | solution.py:12
  87.7 34.4 %all-to-all-done = bf16[32,8,7168]{2,1,0:T(8,128)(2,1)} async-done(((bf16[32,8,7168]{2,1,0:T(8,128)(2,1)}), bf16[32,8,7168]{2,1,0:T(8,128)(2,1)}, u32[]{:S(2)}, u32[]{:S(2)}) %all-to-all-start) | async-done | bytes 3670048 | tf_op jit(solution)/shard_map/all_to_all | solution.py:59
  122.2 6.1 %convolution_convert_fusion = bf16[384,7168]{1,0:T(8,128)(2,1)} fusion(bf16[32,8,7168]{2,1,0:T(8,128)(2,1)} %all-to-all-done, f32[256,384]{1,0:T(8,128)S(1)} %fusion.8, f32[256,384]{1,0:T(8,128)S(1)} %fusion.6), kind=kOutput, calls=%fused_computation | convolution fusion | flops 1412628480 | bytes 9961472 | tf_op jit(solution)/shard_map/dot_general | solution.py:31
  128.3 0.0 reduce-scatter.8.cloned.1.call-update
  128.3 0.2 reduce-scatter.6.cloned.1.call-start
  128.5 5.8 %multiply_convert_fusion.1 = (bf16[256,384]{1,0:T(8,128)(2,1)S(1)}, bf16[256,384]{1,0:T(8,128)(2,1)S(1)}) fusion(f32[256,384]{1,0:T(8,128)S(1)} %fusion.6, f32[256,384]{1,0:T(8,128)S(1)} %fusion.8, bf16[384,7168]{1,0:T(8,128)(2,1)} %param.13, bf16[32,8,7168]{2,1,0:T(8,128)(2,1)} %all-to-all-done), kind=kOutput, calls=%fused_computation.25 | convolution fusion | flops 1410564096 | bytes 10354688 | tf_op jit(solution)/shard_map/dot_general | solution.py:16
  134.3 6.5 %convolution_convert_fusion.1 = bf16[7168,384]{1,0:T(8,128)(2,1)} fusion(bf16[256,384]{1,0:T(8,128)(2,1)S(1)} %get-tuple-element.4, bf16[32,8,7168]{2,1,0:T(8,128)(2,1)} %all-to-all-done.1), kind=kOutput, calls=%fused_computation.1 | convolution fusion | flops 1412038656 | bytes 9371648 | tf_op jit(solution)/shard_map/dot_general | solution.py:30
  140.8 0.0 reduce-scatter.6.cloned.1.call-update
  140.8 0.0 reduce-scatter.4.cloned.1.call-start
  140.9 6.6 %convolution_convert_fusion.2 = bf16[7168,384]{1,0:T(8,128)(2,1)} fusion(bf16[256,384]{1,0:T(8,128)(2,1)S(1)} %get-tuple-element.5, bf16[32,8,7168]{2,1,0:T(8,128)(2,1)} %all-to-all-done.1), kind=kOutput, calls=%fused_computation.2 | convolution fusion | flops 1412038656 | bytes 9371648 | tf_op jit(solution)/shard_map/dot_general | solution.py:29
  147.5 0.0 reduce-scatter.4.cloned.1.call-update
  147.5 4.9 %fusion.23 = f32[256,7168]{1,0:T(8,128)S(1)} fusion(bf16[256,384]{1,0:T(8,128)(2,1)S(1)} %get-tuple-element.5, bf16[7168,384]{1,0:T(8,128)(2,1)} %param.11), kind=kOutput, calls=%fused_computation.40 | convolution fusion | flops 1409286144 | bytes 13041664 | tf_op jit(solution)/shard_map/dot_general | solution.py:22
  152.5 2.1 fusion.1
  154.7 51.9 %all_to_all.15 = bf16[32,8,7168]{2,1,0:T(8,128)(2,1)S(1)} all-to-all(bf16[32,8,7168]{2,1,0:T(8,128)(2,1)S(1)} %fusion.1), channel_id=1, replica_groups=mesh['dp'=4,'expert'=32] {'expert'}, dimensions={0} | all-to-all | bytes 7340032 | tf_op jit(solution)/shard_map/all_to_all | solution.py:64
  206.5 0.5 bitcast_reduce_fusion
  207.1 2.0 fusion.2
  209.1 37.5 %reduce-scatter.6.cloned.1.call-done = bf16[1792,384]{1,0:T(8,128)(2,1)} async-done(((bf16[7168,384]{1,0:T(8,128)(2,1)}), bf16[1792,384]{1,0:T(8,128)(2,1)}) %reduce-scatter.6.cloned.1.call-update) | async-done | bytes 1376272 | tf_op jit(solution)/shard_map/reduce_scatter | solution.py:80
  246.6 60.3 %reduce-scatter.4.cloned.1.call-done = bf16[1792,384]{1,0:T(8,128)(2,1)} async-done(((bf16[7168,384]{1,0:T(8,128)(2,1)}), bf16[1792,384]{1,0:T(8,128)(2,1)}) %reduce-scatter.4.cloned.1.call-update) | async-done | bytes 1376272 | tf_op jit(solution)/shard_map/reduce_scatter | solution.py:77
  (17 shorter events, 0.1 us)
Async XLA Ops:
  7.2 1.5 copy-start
  11.3 9.8 %copy-start.2 = (s32[128,8]{0,1:T(8,128)S(1)}, s32[128,8]{0,1:T(8,128)}, u32[]{:S(2)}) copy-start(s32[128,8]{0,1:T(8,128)} %param.9) | copy-start | bytes 12292
  11.3 9.8 %copy-start.3 = (f32[128,8]{0,1:T(8,128)S(1)}, f32[128,8]{0,1:T(8,128)}, u32[]{:S(2)}) copy-start(f32[128,8]{0,1:T(8,128)} %param.10) | copy-start | bytes 12292
  11.3 55.8 %all-to-all-start.1 = ((bf16[32,8,7168]{2,1,0:T(8,128)(2,1)}), bf16[32,8,7168]{2,1,0:T(8,128)(2,1)}, u32[]{:S(2)}, u32[]{:S(2)}) async-start(bf16[32,8,7168]{2,1,0:T(8,128)(2,1)} %bitcast.41), calls=%async_computation.1 | async-start | bytes 7340032 | tf_op jit(solution)/shard_map/all_to_all | solution.py:58
  69.4 52.8 %all-to-all-start = ((bf16[32,8,7168]{2,1,0:T(8,128)(2,1)}), bf16[32,8,7168]{2,1,0:T(8,128)(2,1)}, u32[]{:S(2)}, u32[]{:S(2)}) async-start(bf16[32,8,7168]{2,1,0:T(8,128)(2,1)} %bitcast.42), calls=%async_computation | async-start | bytes 7340032 | tf_op jit(solution)/shard_map/all_to_all | solution.py:59
  76.2 132.9 %reduce-scatter.8.cloned.1.call-start = ((), (), s32[]{:S(2)}) async-start(), calls=%async_computation.8 | async-start | bytes 6881280 | tf_op jit(solution)/shard_map/reduce_scatter | solution.py:83
  128.3 118.3 %reduce-scatter.6.cloned.1.call-start = ((), (), s32[]{:S(2)}) async-start(), calls=%async_computation.7 | async-start | bytes 6881280 | tf_op jit(solution)/shard_map/reduce_scatter | solution.py:80
  140.8 166.0 %reduce-scatter.4.cloned.1.call-start = ((), (), s32[]{:S(2)}) async-start(), calls=%async_computation.6 | async-start | bytes 6881280 | tf_op jit(solution)/shard_map/reduce_scatter | solution.py:77
  147.5 5.0 %slice-start = ((s8[5505024]{0:T(1024)(128)(4,1)}), s8[1310720]{0:T(1024)(128)(4,1)S(1)}, s32[]{:S(2)}) async-start(s8[5505024]{0:T(1024)(128)(4,1)} %bitcast.43), calls=%async_computation.9 | async-start | bytes 2621440
  147.5 5.0 %slice-start.1 = ((s8[5505024]{0:T(1024)(128)(4,1)}), s8[4194304]{0:T(1024)(128)(4,1)S(1)}, s32[]{:S(2)}) async-start(s8[5505024]{0:T(1024)(128)(4,1)} %bitcast.43), calls=%async_computation.10 | async-start | bytes 8388608
  154.6 152.2 %copy-start.1 = (bf16[128,7168]{1,0:T(8,128)(2,1)S(1)}, bf16[128,7168]{1,0:T(8,128)(2,1)}, u32[]{:S(2)}) copy-start(bf16[128,7168]{1,0:T(8,128)(2,1)} %param.7) | copy-start | bytes 5505028
Sparse Core Ops, SparseCore 0:
  128.4 57.8 reduce-scatter.7
  189.3 57.1 reduce-scatter.5
  249.6 57.2 reduce-scatter.3
where the time goes:
time: 314 us; the launch traced here: 313 us
  waiting for transfers between devices  176 us (56%)
  blocking collectives  51.9 us (17%)
  matrix products  47.8 us (15%)
  starting transfers between devices  16.9 us (5%)
  between operations  13.9 us (4%)
  local copies, waits for them, and re-layouts  4.95 us (2%)
    reduce_scatter x1, waiting for transfers between devices, body(): lax.psum_scatter(g_gate.astype(jnp.bfloat16), 'dp', scatter_dimension=0,...  60.3 us
    all_to_all x1, blocking collectives, body(): lax.all_to_all(back.reshape(peer_count, CAP, width).astype(jnp.bfloat16),...  51.9 us
    all_to_all x1, waiting for transfers between devices, body(): lax.all_to_all(send_in, 'expert', split_axis=0, concat_axis=0, tiled=True)  43.9 us
    reduce_scatter x1, waiting for transfers between devices, body(): lax.psum_scatter(g_up.astype(jnp.bfloat16), 'dp', scatter_dimension=0, ti...  37.5 us
    all_to_all x1, waiting for transfers between devices, body(): lax.all_to_all(send_grad, 'expert', split_axis=0, concat_axis=0, tiled=True)  34.4 us
    all_to_all x1, starting transfers between devices, body(): lax.all_to_all(send_in, 'expert', split_axis=0, concat_axis=0, tiled=True)  9.78 us
    all_to_all x1, starting transfers between devices, body(): lax.all_to_all(send_grad, 'expert', split_axis=0, concat_axis=0, tiled=True)  6.79 us
    dot_general x1, matrix products, weight_terms(): lax.dot_general(rows_in, d_gate, contract_rows, preferred_element_type=jn...  6.6 us
  transfers between devices with their start and end apart: 5, of which 4 were waited for; matrix products, arithmetic and copies ran while one was open for 13% of the time, Pallas kernels for 0%

commit v1 on v0

v1 whole, which is shorter than its diff:
```python
import jax
import jax.numpy as jnp
from jax import lax
from jax.experimental import pallas as pl
from jax.experimental.pallas import tpu as pltpu
from jax.sharding import PartitionSpec as P

CAP = 8
CHIPS = 16
DP = 4
NCH = 2
KCH = 1024
NB = 256
MESH = pl.DeviceIdType.MESH


def kernel(
    send, pick, wg, wu, wd,
    gt, gg, gu, gd,
    recv, wgu, wdv, xbuf, dall, gu_acc, dh_acc, ret, sib, fin, hid_t, sb,
    w_sem, loc_sem, locx_sem, ds_sem, dr_sem, fs_sem, fr_sem, xs_sem, xr_sem, xfs_sem, xfr_sem,
    gs_sem, gr_sem, ss_sem, sr_sem, rs_sem, rr_sem,
):
    width = wdv.shape[1]
    hid = wdv.shape[0]
    quarter = width // DP
    half = width // 2
    part = half // NCH
    x = lax.axis_index("dp")
    idx = lax.axis_index("expert")
    k = lax.rem(idx, 2)
    chip = idx // 2
    y = chip // 4
    z = lax.rem(chip, 4)
    sibling = (x, chip * 2 + (1 - k))
    mine = k * CHIPS
    other = (1 - k) * CHIPS

    loads = [
        pltpu.make_async_copy(wg, wgu.at[:, pl.ds(0, hid)], w_sem.at[0]),
        pltpu.make_async_copy(wu, wgu.at[:, pl.ds(hid, hid)], w_sem.at[1]),
        pltpu.make_async_copy(wd, wdv, w_sem.at[2]),
    ]

    barrier = pltpu.get_barrier_semaphore()

    def greet(o, carry):
        peer = lax.rem(chip + o, CHIPS)
        pl.semaphore_signal(barrier, inc=1, device_id=(x, peer * 2 + k), device_id_type=MESH)
        return carry

    lax.fori_loop(1, CHIPS, greet, 0)
    for d in range(1, DP):
        pl.semaphore_signal(barrier, inc=1, device_id=(lax.rem(x + d, DP), idx), device_id_type=MESH)
    pl.semaphore_signal(barrier, inc=1, device_id=sibling, device_id_type=MESH)
    pl.semaphore_wait(barrier, CHIPS - 1 + DP - 1 + 1)

    def chip_at(dy, dz, sign):
        return lax.rem(y + sign * dy + 4, 4) * 4 + lax.rem(z + sign * dz + 4, 4)

    def dispatch(dy, dz):
        to = chip_at(dy, dz, 1)
        return pltpu.make_async_remote_copy(
            src_ref=send.at[to // 2],
            dst_ref=recv.at[mine + chip],
            send_sem=ds_sem.at[dy * 4 + dz],
            recv_sem=dr_sem.at[dy * 4 + dz],
            device_id=(x, to * 2 + k),
            device_id_type=MESH,
        )

    own = pltpu.make_async_copy(send.at[chip // 2], recv.at[mine + chip], loc_sem)
    for dy in range(4):
        for dz in range(4):
            if dy == 0 and dz == 0:
                own.start()
            else:
                dispatch(dy, dz).start()
    for load in loads:
        load.start()

    def forward(dy):
        at = pl.ds(mine + lax.rem(y - dy + 4, 4) * 4, 4)
        return pltpu.make_async_remote_copy(
            src_ref=recv.at[at], dst_ref=recv.at[at],
            send_sem=fs_sem.at[dy], recv_sem=fr_sem.at[dy],
            device_id=sibling, device_id_type=MESH,
        )

    def exchange(dy, d):
        at = pl.ds(mine + lax.rem(y - dy + 4, 4) * 4, 4)
        to = lax.rem(x + d, DP)
        columns = pl.ds(pl.multiple_of(to * quarter, 128), quarter)
        return pltpu.make_async_remote_copy(
            src_ref=recv.at[at, :, columns], dst_ref=xbuf.at[x, at],
            send_sem=xs_sem.at[dy * 3 + d - 1], recv_sem=xr_sem.at[dy * 3 + d - 1],
            device_id=(to, idx), device_id_type=MESH,
        )

    def exchange_forward(dy, d):
        at = pl.ds(mine + lax.rem(y - dy + 4, 4) * 4, 4)
        source = lax.rem(x - d + DP, DP)
        return pltpu.make_async_remote_copy(
            src_ref=xbuf.at[source, at], dst_ref=xbuf.at[source, at],
            send_sem=xfs_sem.at[dy * 3 + d - 1], recv_sem=xfr_sem.at[dy * 3 + d - 1],
            device_id=sibling, device_id_type=MESH,
        )

    for dy in range(4):
        for dz in range(4):
            if dy == 0 and dz == 0:
                own.wait()
            else:
                dispatch(dy, dz).wait_recv()
        forward(dy).start()
        for d in range(1, DP):
            exchange(dy, d).start()
        if dy > 0:
            for d in range(1, DP):
                exchange(dy - 1, d).wait_recv()
                exchange_forward(dy - 1, d).start()
    for dy in range(4):
        forward(dy).wait_recv()
    keep = pltpu.make_async_copy(
        recv.at[:, :, pl.ds(pl.multiple_of(x * quarter, 128), quarter)], xbuf.at[x], locx_sem
    )
    keep.start()
    for load in loads:
        load.wait()

    def flat(block, rows):
        return block.astype(jnp.float32).reshape(rows, block.shape[-1]).astype(jnp.bfloat16)

    gu_acc[...] = jnp.zeros_like(gu_acc)
    dh_acc[...] = jnp.zeros_like(dh_acc)

    def contract(i, carry):
        at = pl.ds(pl.multiple_of(i * KCH, KCH), KCH)
        rows_in = flat(recv[:, pl.ds(0, CAP), at], 256)
        rows_grad = flat(recv[:, pl.ds(CAP, CAP), at], 256)
        gu_acc[...] += jnp.dot(rows_in, wgu[at, :], preferred_element_type=jnp.float32)
        dh_acc[...] += lax.dot_general(
            rows_grad, wdv[:, at], (((1,), (1,)), ((), ())), preferred_element_type=jnp.float32
        )
        return carry

    lax.fori_loop(0, width // KCH, contract, 0)

    gate_pre = gu_acc[:, :hid]
    up_pre = gu_acc[:, hid:]
    d_hidden = dh_acc[...]
    sig = jax.nn.sigmoid(gate_pre)
    act = gate_pre * sig
    dall[x, :, pl.ds(0, hid)] = (
        d_hidden * up_pre * sig * (1.0 + gate_pre * (1.0 - sig))
    ).astype(jnp.bfloat16)
    dall[x, :, pl.ds(hid, hid)] = (d_hidden * act).astype(jnp.bfloat16)
    dall[x, :, pl.ds(2 * hid, hid)] = (act * up_pre).astype(jnp.bfloat16)

    def gather(d):
        return pltpu.make_async_remote_copy(
            src_ref=dall.at[x], dst_ref=dall.at[x],
            send_sem=gs_sem.at[d - 1], recv_sem=gr_sem.at[d - 1],
            device_id=(lax.rem(x + d, DP), idx), device_id_type=MESH,
        )

    for d in range(1, DP):
        gather(d).start()

    def to_sibling(q):
        return pltpu.make_async_remote_copy(
            src_ref=ret.at[pl.ds(other, CHIPS), :, pl.ds(q * part, part)],
            dst_ref=sib.at[:, :, pl.ds(q * part, part)],
            send_sem=ss_sem.at[q], recv_sem=sr_sem.at[q],
            device_id=sibling, device_id_type=MESH,
        )

    def give_back(q, dy, dz):
        to = chip_at(dy, dz, 1)
        return pltpu.make_async_remote_copy(
            src_ref=ret.at[mine + to, :, pl.ds(q * part, part)],
            dst_ref=fin.at[chip, :, pl.ds(q * part, part)],
            send_sem=rs_sem.at[q * 16 + dy * 4 + dz], recv_sem=rr_sem.at[q * 16 + dy * 4 + dz],
            device_id=(x, to * 2 + k), device_id_type=MESH,
        )

    def keep_back(q):
        return pltpu.make_async_copy(
            ret.at[mine + chip, :, pl.ds(q * part, part)],
            fin.at[chip, :, pl.ds(q * part, part)],
            rs_sem.at[q * 16],
        )

    for q in range(NCH):
        for h in range(2):
            def back(i, carry, q=q, h=h):
                col = pl.multiple_of(q * part + i * NB, NB)
                out = lax.dot_general(
                    dall[x, :, pl.ds(0, 2 * hid)],
                    wgu[pl.ds(pl.multiple_of(h * half + col, NB), NB), :],
                    (((1,), (1,)), ((), ())),
                    preferred_element_type=jnp.float32,
                )
                ret[:, pl.ds(h * CAP, CAP), pl.ds(col, NB)] = out.reshape(
                    2 * CHIPS, CAP, NB
                ).astype(jnp.bfloat16)
                return carry

            lax.fori_loop(0, part // NB, back, 0)
        to_sibling(q).start()

    for q in range(NCH):
        to_sibling(q).wait_recv()

        def add(i, carry, q=q):
            at = pl.ds(q * part, part)
            ret[mine + i, :, at] = (
                ret[mine + i, :, at].astype(jnp.float32) + sib[i, :, at].astype(jnp.float32)
            ).astype(jnp.bfloat16)
            return carry

        lax.fori_loop(0, CHIPS, add, 0)
        for dy in range(4):
            for dz in range(4):
                if dy == 0 and dz == 0:
                    keep_back(q).start()
                else:
                    give_back(q, dy, dz).start()

    for d in range(1, DP):
        exchange(3, d).wait_recv()
        exchange_forward(3, d).start()
    keep.wait()
    for d in range(1, DP):
        gather(d).wait_recv()
    for dy in range(4):
        for d in range(1, DP):
            exchange_forward(dy, d).wait_recv()
    rows = DP * 2 * CHIPS * CAP
    hid_t[...] = dall[:, :, pl.ds(2 * hid, hid)].reshape(rows, hid).T

    def weights(i, carry):
        at = pl.ds(pl.multiple_of(i * NB, NB), NB)
        rows_in = flat(xbuf[:, :, pl.ds(0, CAP), at], rows)
        rows_grad = flat(xbuf[:, :, pl.ds(CAP, CAP), at], rows)
        out = jnp.dot(
            rows_in.T,
            dall[:, :, pl.ds(0, 2 * hid)].reshape(rows, 2 * hid),
            preferred_element_type=jnp.float32,
        )
        gg[at, :] = out[:, :hid].astype(jnp.bfloat16)
        gu[at, :] = out[:, hid:].astype(jnp.bfloat16)
        gd[:, at] = jnp.dot(hid_t[...], rows_grad, preferred_element_type=jnp.float32).astype(
            jnp.bfloat16
        )
        return carry

    lax.fori_loop(0, quarter // NB, weights, 0)

    for q in range(NCH):
        for dy in range(4):
            for dz in range(4):
                if dy == 0 and dz == 0:
                    keep_back(q).wait()
                else:
                    give_back(q, dy, dz).wait_recv()
    pick_v = pick[...]
    for h in range(2):
        def combine(i, carry, h=h):
            col = pl.multiple_of(i * NB, NB)
            for e in range(CHIPS // 2):
                sb[pl.ds(e * CAP, CAP), :] = (
                    fin[2 * e, pl.ds(h * CAP, CAP), pl.ds(col, NB)].astype(jnp.float32)
                    + fin[2 * e + 1, pl.ds(h * CAP, CAP), pl.ds(col, NB)].astype(jnp.float32)
                )
            gt[:, pl.ds(pl.multiple_of(h * half + col, NB), NB)] = jnp.dot(
                pick_v, sb[...].astype(jnp.bfloat16), preferred_element_type=jnp.float32
            ).astype(jnp.bfloat16)
            return carry

        lax.fori_loop(0, half // NB, combine, 0)

    for dy in range(4):
        forward(dy).wait_send()
        for d in range(1, DP):
            exchange(dy, d).wait_send()
            exchange_forward(dy, d).wait_send()
        for dz in range(4):
            if dy or dz:
                dispatch(dy, dz).wait_send()
                for q in range(NCH):
                    give_back(q, dy, dz).wait_send()
    for d in range(1, DP):
        gather(d).wait_send()
    for q in range(NCH):
        to_sibling(q).wait_send()


def body(tokens, grad_out, expert_ids, gate_weights, w_gate, w_up, w_down):
    experts = CHIPS // 2
    width = tokens.shape[1]
    hid = w_gate.shape[1]
    half = width // 2
    quarter = width // DP
    chosen = expert_ids[None, :, :] == jnp.arange(experts, dtype=jnp.int32)[:, None, None]
    member = jnp.sum(chosen.astype(jnp.int32), axis=2)
    weight = jnp.sum(jnp.where(chosen, gate_weights[None, :, :], jnp.float32(0.0)), axis=2)
    position = jnp.cumsum(member, axis=1) - 1
    slot_mask = (member[..., None] == 1) & (position[..., None] == jnp.arange(CAP, dtype=jnp.int32))
    picker = slot_mask.astype(jnp.bfloat16)
    slot_inputs = jnp.einsum(
        "etc,td->ecd", picker, tokens, preferred_element_type=jnp.float32
    ).astype(jnp.bfloat16)
    raw_grads = jnp.einsum("etc,td->ecd", picker, grad_out, preferred_element_type=jnp.float32)
    slot_gate = jnp.sum(slot_mask.astype(jnp.float32) * weight[..., None], axis=1)
    slot_grads = (slot_gate[..., None] * raw_grads).astype(jnp.bfloat16)
    send = jnp.concatenate([slot_inputs, slot_grads], axis=1)
    pick = jnp.transpose(picker, (1, 0, 2)).reshape(tokens.shape[0], experts * CAP)
    any_spec = pl.BlockSpec(memory_space=pl.ANY)
    vmem = pl.BlockSpec(memory_space=pltpu.VMEM)
    bf16 = jnp.bfloat16
    dma = pltpu.SemaphoreType.DMA
    return pl.pallas_call(
        kernel,
        out_shape=(
            jax.ShapeDtypeStruct(tokens.shape, bf16),
            jax.ShapeDtypeStruct((quarter, hid), bf16),
            jax.ShapeDtypeStruct((quarter, hid), bf16),
            jax.ShapeDtypeStruct((hid, quarter), bf16),
        ),
        in_specs=[any_spec, vmem, any_spec, any_spec, any_spec],
        out_specs=(vmem, vmem, vmem, vmem),
        scratch_shapes=[
            pltpu.VMEM((2 * CHIPS, 2 * CAP, width), bf16),
            pltpu.VMEM((width, 2 * hid), bf16),
            pltpu.VMEM((hid, width), bf16),
            pltpu.VMEM((DP, 2 * CHIPS, 2 * CAP, quarter), bf16),
            pltpu.VMEM((DP, 2 * CHIPS * CAP, 3 * hid), bf16),
            pltpu.VMEM((2 * CHIPS * CAP, 2 * hid), jnp.float32),
            pltpu.VMEM((2 * CHIPS * CAP, hid), jnp.float32),
            pltpu.VMEM((2 * CHIPS, 2 * CAP, half), bf16),
            pltpu.VMEM((CHIPS, 2 * CAP, half), bf16),
            pltpu.VMEM((CHIPS, 2 * CAP, half), bf16),
            pltpu.VMEM((hid, DP * 2 * CHIPS * CAP), bf16),
            pltpu.VMEM((experts * CAP, NB), jnp.float32),
            dma((3,)), dma, dma,
            dma((16,)), dma((16,)),
            dma((4,)), dma((4,)),
            dma((12,)), dma((12,)), dma((12,)), dma((12,)),
            dma((3,)), dma((3,)),
            dma((NCH,)), dma((NCH,)),
            dma((16 * NCH,)), dma((16 * NCH,)),
        ],
        compiler_params=pltpu.CompilerParams(
            collective_id=0, has_side_effects=True, vmem_limit_bytes=60 * 1024 * 1024
        ),
        cost_estimate=pl.CostEstimate(
            flops=8 * 2 * 256 * width * hid, bytes_accessed=26_000_000, transcendentals=256 * hid
        ),
    )(send, pick, w_gate, w_up, w_down)


def solution(mesh):
    in_specs = (
        P(("dp", "expert"), None),
        P(("dp", "expert"), None),
        P(("dp", "expert"), None),
        P(("dp", "expert"), None),
        P(None, "expert"),
        P(None, "expert"),
        P("expert", None),
    )
    out_specs = (P(("dp", "expert"), None), P("dp", "expert"), P("dp", "expert"), P("expert", "dp"))
    return jax.shard_map(body, mesh=mesh, in_specs=in_specs, out_specs=out_specs, check_vma=False)
```

time: 314 us -> 144 us (0.46)
  the two profiles are of different devices: /device:TPU:1 before, /device:TPU:8 now
where the time goes in v1:
time: 144 us
  Pallas kernels  130 us (90%)
  local copies, waits for them, and re-layouts  8.5 us (6%)
  other arithmetic  3.92 us (3%)
    pallas_call x1, Pallas kernels, body(): pl.pallas_call(kernel, out_shape=(jax.ShapeDtypeStruct(tokens.shape, bf16...  130 us
    unnamed x14, local copies, waits for them, and re-layouts  8.19 us

profile of v1, /device:TPU:8, one launch (start us, length us, event | category | flops | bytes accessed | tf_op | source)
XLA Modules:
  0.0 144.1 jit_solution(10085662682935323593)
XLA Ops:
  0.6 0.0 copy-start
  0.6 0.8 convert_reduce_fusion
  1.5 0.3 reduce_window_sum.11
  1.8 0.1 eq.67
  1.9 0.8 fusion.18
  2.7 0.1 copy.17
  2.8 0.1 copy.15
  2.9 0.0 copy-start.1
  2.9 0.6 and_convert_fusion.pick
  3.6 0.0 copy-done
  3.6 0.4 fusion.1
  4.0 0.5 copy-done.1
  4.4 0.4 convolution_convert_fusion
  4.9 1.4 pad_maximum_fusion.send
  6.2 130.1 %shard_map.102 = (bf16[128,7168]{1,0:T(8,128)(2,1)}, bf16[1792,384]{1,0:T(8,128)(2,1)}, bf16[1792,384]{1,0:T(8,128)(2,1)}, bf16[384,1792]{1,0:T(8,128)(2,1)}) custom-call(bf16[8,16,7168]{2,1,0:T(8,128)(2,1)} %pad_maximum_fusion.send, bf16[128,64]{1,0:T(8,128)(2,1)} %and_convert_fusion.pick, bf16[7168,384]{1,0:T(8,128)(2,1)} %wg.1, bf16[7168,384]{1,0:T(8,128)(2,1)} %wu.1, ...), custom_call_target="tpu_custom_call" | custom-call | flops 11274289152 | bytes 26000000 | tf_op jit(solution)/shard_map/pallas_call | solution.py:323
  136.4 0.0 copy-start.4
  136.4 3.0 %copy.22 = bf16[128,7168]{1,0:T(8,128)(2,1)} copy(bf16[128,7168]{1,0:T(8,128)(2,1)} %get-tuple-element.10) | data formatting | bytes 3670016
  139.3 0.0 copy-done.4
  139.3 0.0 copy-start.3
  139.3 1.1 copy.23
  140.4 0.8 copy-done.3
  141.2 0.0 copy-start.2
  141.2 1.1 copy.24
  142.2 0.8 copy-done.2
  143.0 1.1 copy.25
  (6 shorter events, 0.0 us)
Async XLA Ops:
  0.6 2.9 %copy-start = (bf16[128,7168]{1,0:T(8,128)(2,1)S(1)}, bf16[128,7168]{1,0:T(8,128)(2,1)}, u32[]{:S(2)}) copy-start(bf16[128,7168]{1,0:T(8,128)(2,1)} %param.8) | copy-start | bytes 5505028
  2.9 1.5 %copy-start.1 = (bf16[128,7168]{1,0:T(8,128)(2,1)S(1)}, bf16[128,7168]{1,0:T(8,128)(2,1)}, u32[]{:S(2)}) copy-start(bf16[128,7168]{1,0:T(8,128)(2,1)} %param.7) | copy-start | bytes 5505028
  136.4 3.0 %copy-start.4 = (bf16[1792,384]{1,0:T(8,128)(2,1)S(1)}, bf16[1792,384]{1,0:T(8,128)(2,1)}, u32[]{:S(2)}) copy-start(bf16[1792,384]{1,0:T(8,128)(2,1)} %get-tuple-element.11) | copy-start | bytes 4128772
  139.3 1.8 %copy-start.3 = (bf16[1792,384]{1,0:T(8,128)(2,1)S(1)}, bf16[1792,384]{1,0:T(8,128)(2,1)}, u32[]{:S(2)}) copy-start(bf16[1792,384]{1,0:T(8,128)(2,1)} %get-tuple-element.12) | copy-start | bytes 4128772
  141.2 1.8 %copy-start.2 = (bf16[384,1792]{1,0:T(8,128)(2,1)S(1)}, bf16[384,1792]{1,0:T(8,128)(2,1)}, u32[]{:S(2)}) copy-start(bf16[384,1792]{1,0:T(8,128)(2,1)} %get-tuple-element.13) | copy-start | bytes 4128772

commit v2 on v0

v2 whole, which is shorter than its diff:
```python
import jax
import jax.numpy as jnp
from jax import lax
from jax.experimental import pallas as pl
from jax.experimental.pallas import tpu as pltpu
from jax.sharding import PartitionSpec as P

CAP = 8
ROW = 2 * CAP
DP = 4
EXPERTS = 8
BLOCKS = 32
DY = (0, 1, 3, 2)
PASSES = 2
PER_PASS = len(DY) // PASSES
KCH = 1024
NB = 512
MESH = pl.DeviceIdType.MESH


def flat(block):
    wide = block.astype(jnp.float32).reshape(block.shape[0] * block.shape[1], block.shape[2])
    return wide.astype(jnp.bfloat16)


def exchange_kernel(
    send, wg, wu, wd,
    xbuf, dall, fin,
    recv, mid, wgu, wdv, dloc, gu_acc, dh_acc, ret, sib, zin, zsum,
    w_sem, own_sem, keep_sem, dk_sem, fk_sem,
    ys_sem, yr_sem, zs_sem, zr_sem, fs_sem, fr_sem, xs_sem, xr_sem, xfs_sem, xfr_sem,
    gs_sem, gr_sem, ss_sem, sr_sem, rs_sem, rr_sem, bs_sem, br_sem,
):
    hid, width = wdv.shape
    quarter = width // DP
    x = lax.axis_index("dp")
    idx = lax.axis_index("expert")
    k = lax.rem(idx, 2)
    chip = idx // 2
    y = chip // 4
    z = lax.rem(chip, 4)
    pair = z // 2
    zs = (2 * pair + (1 - lax.rem(z, 2)), 3 - z, lax.rem(z + 2, 4))

    def device(yy, zz, kk):
        return (x, (yy * 4 + zz) * 2 + kk)

    def remote(src, dst, send_sem, recv_sem, to):
        return pltpu.make_async_remote_copy(
            src_ref=src, dst_ref=dst, send_sem=send_sem, recv_sem=recv_sem,
            device_id=to, device_id_type=MESH,
        )

    ahead = [lax.rem(y + dy, 4) for dy in DY]
    behind = [lax.rem(y - dy + 4, 4) for dy in DY]
    sibling = device(y, z, 1 - k)
    peers = [(lax.rem(x + d, DP), idx) for d in range(1, DP)]
    sources = [lax.rem(x - d + DP, DP) for d in range(1, DP)]

    barrier = pltpu.get_barrier_semaphore()
    near = [device(ahead[g], z, k) for g in (1, 2, 3)] + [device(y, t, k) for t in zs]
    for to in near + peers + [sibling]:
        pl.semaphore_signal(barrier, inc=1, device_id=to, device_id_type=MESH)
    pl.semaphore_wait(barrier, 10)

    def own_block(g, zz):
        return g * 8 + k * 4 + zz

    def along_y(g, far):
        expert = 2 * ahead[g] + (1 - pair if far else pair)
        return remote(
            send.at[expert],
            mid.at[g - 1] if far else recv.at[own_block(g, z)],
            ys_sem.at[g * 2 + far], yr_sem.at[g * 2 + far], device(ahead[g], z, k),
        )

    def along_z(g, t):
        if t == 0:
            src = send.at[2 * y + pair] if g == 0 else recv.at[own_block(g, z)]
        else:
            src = send.at[2 * y + 1 - pair] if g == 0 else mid.at[g - 1]
        return remote(
            src, recv.at[own_block(g, z)],
            zs_sem.at[g * 3 + t], zr_sem.at[g * 3 + t], device(y, zs[t], k),
        )

    def z_arrival(g, t):
        at = recv.at[own_block(g, zs[t])]
        return remote(at, at, zs_sem.at[g * 3 + t], zr_sem.at[g * 3 + t], device(y, zs[t], k))

    own = pltpu.make_async_copy(send.at[2 * y + pair], recv.at[own_block(0, z)], own_sem)
    loads = [
        pltpu.make_async_copy(wg, wgu.at[:, pl.ds(0, hid)], w_sem.at[0]),
        pltpu.make_async_copy(wu, wgu.at[:, pl.ds(hid, hid)], w_sem.at[1]),
        pltpu.make_async_copy(wd, wdv, w_sem.at[2]),
    ]

    def forward(g):
        at = recv.at[pl.ds(own_block(g, 0), 4)]
        return remote(at, at, fs_sem.at[g], fr_sem.at[g], sibling)

    def exchange(g, d):
        to = peers[d][0]
        columns = pl.ds(pl.multiple_of(to * quarter, 128), quarter)
        at = pl.ds(own_block(g, 0), 4)
        return remote(
            recv.at[at, :, columns], xbuf.at[x, at],
            xs_sem.at[g * 3 + d], xr_sem.at[g * 3 + d], peers[d],
        )

    def exchange_forward(g, d):
        at = xbuf.at[sources[d], pl.ds(own_block(g, 0), 4)]
        return remote(at, at, xfs_sem.at[g * 3 + d], xfr_sem.at[g * 3 + d], sibling)

    def keep(p):
        at = pl.ds(p * 8 * PER_PASS, 8 * PER_PASS)
        columns = pl.ds(pl.multiple_of(x * quarter, 128), quarter)
        return pltpu.make_async_copy(recv.at[at, :, columns], xbuf.at[x, at], keep_sem.at[p])

    rows = PER_PASS * 8 * CAP

    def gather(p, d):
        at = pl.ds(p * rows, rows)
        return remote(
            dloc.at[at], dall.at[x, at], gs_sem.at[p * 3 + d], gr_sem.at[p * 3 + d], peers[d]
        )

    def keep_terms(p):
        at = pl.ds(p * rows, rows)
        return pltpu.make_async_copy(dloc.at[at], dall.at[x, at], dk_sem.at[p])

    def relay(g):
        for far in (0, 1):
            along_y(g, far).wait_recv()
        for t in range(3):
            along_z(g, t).start()

    def arrive(g):
        if g == 0:
            own.wait()
        for t in range(3):
            z_arrival(g, t).wait_recv()
        forward(g).start()
        for d in range(3):
            exchange(g, d).start()

    def exchanged(g):
        for d in range(3):
            exchange(g, d).wait_recv()
            exchange_forward(g, d).start()

    def terms(p):
        for g in range(p * PER_PASS, (p + 1) * PER_PASS):
            forward(g).wait_recv()
        keep(p).start()
        blocks = pl.ds(p * 8 * PER_PASS, 8 * PER_PASS)
        gu_acc[...] = jnp.zeros_like(gu_acc)
        dh_acc[...] = jnp.zeros_like(dh_acc)

        def contract(i, carry):
            at = pl.ds(pl.multiple_of(i * KCH, KCH), KCH)
            gu_acc[...] += jnp.dot(
                flat(recv[blocks, pl.ds(0, CAP), at]), wgu[at, :],
                preferred_element_type=jnp.float32,
            )
            dh_acc[...] += lax.dot_general(
                flat(recv[blocks, pl.ds(CAP, CAP), at]), wdv[:, at],
                (((1,), (1,)), ((), ())), preferred_element_type=jnp.float32,
            )
            return carry

        lax.fori_loop(0, width // KCH, contract, 0)
        gate_pre = gu_acc[:, :hid]
        up_pre = gu_acc[:, hid:]
        d_hidden = dh_acc[...]
        sig = jax.nn.sigmoid(gate_pre)
        act = gate_pre * sig
        at = pl.ds(p * rows, rows)
        dloc[at, pl.ds(0, hid)] = (
            d_hidden * up_pre * sig * (1.0 + gate_pre * (1.0 - sig))
        ).astype(jnp.bfloat16)
        dloc[at, pl.ds(hid, hid)] = (d_hidden * act).astype(jnp.bfloat16)
        dloc[at, pl.ds(2 * hid, hid)] = (act * up_pre).astype(jnp.bfloat16)
        for d in range(3):
            gather(p, d).start()
        keep_terms(p).start()

    def to_sibling(g):
        return remote(
            ret.at[pl.ds(g * 8 + (1 - k) * 4, 4)], sib.at[pl.ds(g * 4, 4)],
            ss_sem.at[g], sr_sem.at[g], sibling,
        )

    def back(p):
        def columns(b, carry):
            for h in range(2):
                out = lax.dot_general(
                    dloc[pl.ds(p * rows, rows), pl.ds(0, 2 * hid)],
                    wgu[pl.ds(pl.multiple_of(b * 2 * NB + h * NB, NB), NB), :],
                    (((1,), (1,)), ((), ())),
                    preferred_element_type=jnp.float32,
                )
                ret[
                    pl.ds(p * 8 * PER_PASS, 8 * PER_PASS), pl.ds(h * CAP, CAP),
                    pl.ds(pl.multiple_of(b * NB, NB), NB),
                ] = out.reshape(8 * PER_PASS, CAP, NB).astype(jnp.bfloat16)
            return carry

        lax.fori_loop(0, width // (2 * NB), columns, 0)
        for g in range(p * PER_PASS, (p + 1) * PER_PASS):
            to_sibling(g).start()

    def return_z(g, t):
        return remote(
            ret.at[own_block(g, zs[t])], zin.at[g * 4 + z],
            rs_sem.at[g * 3 + t], rr_sem.at[g * 3 + t], device(y, zs[t], k),
        )

    def return_arrival(g, t):
        at = zin.at[g * 4 + zs[t]]
        return remote(at, at, rs_sem.at[g * 3 + t], rr_sem.at[g * 3 + t], device(y, zs[t], k))

    def plus(a, b):
        return (a.astype(jnp.float32) + b.astype(jnp.float32)).astype(jnp.bfloat16)

    def give_back(p):
        for g in range(p * PER_PASS, (p + 1) * PER_PASS):
            to_sibling(g).wait_recv()

            def add(i, carry, g=g):
                at = own_block(g, i)
                ret[at] = plus(ret[at], sib[g * 4 + i])
                return carry

            lax.fori_loop(0, 4, add, 0)
            for t in range(3):
                return_z(g, t).start()
            zin[g * 4 + z] = ret[own_block(g, z)]

    def return_y(g):
        return remote(
            zsum.at[pl.ds(2 * g, 2)], fin.at[pl.ds(2 * y, 2)],
            bs_sem.at[g], br_sem.at[g], device(behind[g], z, k),
        )

    home = pltpu.make_async_copy(zsum.at[pl.ds(0, 2)], fin.at[pl.ds(2 * y, 2)], fk_sem)

    def relay_back(p):
        for g in range(p * PER_PASS, (p + 1) * PER_PASS):
            for t in range(3):
                return_arrival(g, t).wait_recv()

            def add(i, carry, g=g):
                zsum[2 * g + i] = plus(zin[g * 4 + 2 * i], zin[g * 4 + 2 * i + 1])
                return carry

            lax.fori_loop(0, 2, add, 0)
            if g == 0:
                home.start()
            else:
                return_y(g).start()

    own.start()
    for t in range(3):
        along_z(0, t).start()
    for g in (1, 2):
        for far in (0, 1):
            along_y(g, far).start()
    for load in loads:
        load.start()
    relay(1)
    for far in (0, 1):
        along_y(3, far).start()
    arrive(0)
    relay(2)
    arrive(1)
    relay(3)
    for load in loads:
        load.wait()
    terms(0)
    back(0)
    arrive(2)
    exchanged(0)
    arrive(3)
    exchanged(1)
    give_back(0)
    terms(1)
    relay_back(0)
    back(1)
    exchanged(2)
    give_back(1)
    exchanged(3)
    relay_back(1)

    for g in range(4):
        for d in range(3):
            exchange_forward(g, d).wait_recv()
    for p in range(PASSES):
        keep(p).wait()
        keep_terms(p).wait()
        for d in range(3):
            gather(p, d).wait()
    home.wait()
    for g in range(1, 4):
        return_y(g).wait()
        for far in (0, 1):
            along_y(g, far).wait_send()
    for g in range(4):
        for t in range(3):
            along_z(g, t).wait_send()
            return_z(g, t).wait_send()
        for d in range(3):
            exchange(g, d).wait_send()
            exchange_forward(g, d).wait_send()
        forward(g).wait_send()
        to_sibling(g).wait_send()


def finish_kernel(xbuf, dall, fin, pick, gt, gg, gu, gd, hid_t):
    rows = dall.shape[0] * dall.shape[1]
    hid = dall.shape[2] // 3

    @pl.when(pl.program_id(0) == 0)
    def _():
        hid_t[...] = dall[:, :, 2 * hid:].reshape(rows, hid).T

    rows_in = flat(xbuf[:, pl.ds(0, CAP), :])
    rows_grad = flat(xbuf[:, pl.ds(CAP, CAP), :])
    out = jnp.dot(
        rows_in.T, dall[:, :, : 2 * hid].reshape(rows, 2 * hid), preferred_element_type=jnp.float32
    )
    gg[...] = out[:, :hid].astype(jnp.bfloat16)
    gu[...] = out[:, hid:].astype(jnp.bfloat16)
    gd[...] = jnp.dot(hid_t[...], rows_grad, preferred_element_type=jnp.float32).astype(jnp.bfloat16)
    for h in range(2):
        gt[:, pl.ds(h * NB, NB)] = jnp.dot(
            pick[...], flat(fin[:, pl.ds(h * CAP, CAP), :]), preferred_element_type=jnp.float32
        ).astype(jnp.bfloat16)


def body(tokens, grad_out, expert_ids, gate_weights, w_gate, w_up, w_down):
    width = tokens.shape[1]
    hid = w_gate.shape[1]
    half = width // 2
    quarter = width // DP
    slots = BLOCKS * CAP
    chosen = expert_ids[None, :, :] == jnp.arange(EXPERTS, dtype=jnp.int32)[:, None, None]
    member = jnp.sum(chosen.astype(jnp.int32), axis=2)
    weight = jnp.sum(jnp.where(chosen, gate_weights[None, :, :], jnp.float32(0.0)), axis=2)
    position = jnp.cumsum(member, axis=1) - 1
    slot_mask = (member[..., None] == 1) & (position[..., None] == jnp.arange(CAP, dtype=jnp.int32))
    picker = slot_mask.astype(jnp.bfloat16)
    slot_inputs = jnp.einsum(
        "etc,td->ecd", picker, tokens, preferred_element_type=jnp.float32
    ).astype(jnp.bfloat16)
    raw_grads = jnp.einsum("etc,td->ecd", picker, grad_out, preferred_element_type=jnp.float32)
    slot_gate = jnp.sum(slot_mask.astype(jnp.float32) * weight[..., None], axis=1)
    slot_grads = (slot_gate[..., None] * raw_grads).astype(jnp.bfloat16)
    send = jnp.concatenate([slot_inputs, slot_grads], axis=1)
    pick = jnp.transpose(picker, (1, 0, 2)).reshape(tokens.shape[0], EXPERTS * CAP)
    any_spec = pl.BlockSpec(memory_space=pl.ANY)
    bf16 = jnp.bfloat16
    dma = pltpu.SemaphoreType.DMA
    groups = len(DY)
    xbuf, dall, fin = pl.pallas_call(
        exchange_kernel,
        out_shape=(
            jax.ShapeDtypeStruct((DP, BLOCKS, ROW, quarter), bf16),
            jax.ShapeDtypeStruct((DP, slots, 3 * hid), bf16),
            jax.ShapeDtypeStruct((EXPERTS, ROW, half), bf16),
        ),
        in_specs=[any_spec] * 4,
        out_specs=(any_spec,) * 3,
        scratch_shapes=[
            pltpu.VMEM((BLOCKS, ROW, width), bf16),
            pltpu.VMEM((3, ROW, width), bf16),
            pltpu.VMEM((width, 2 * hid), bf16),
            pltpu.VMEM((hid, width), bf16),
            pltpu.VMEM((slots, 3 * hid), bf16),
            pltpu.VMEM((slots // PASSES, 2 * hid), jnp.float32),
            pltpu.VMEM((slots // PASSES, hid), jnp.float32),
            pltpu.VMEM((BLOCKS, ROW, half), bf16),
            pltpu.VMEM((BLOCKS // 2, ROW, half), bf16),
            pltpu.VMEM((BLOCKS // 2, ROW, half), bf16),
            pltpu.VMEM((EXPERTS, ROW, half), bf16),
            dma((3,)), dma, dma((PASSES,)), dma((PASSES,)), dma,
            dma((8,)), dma((8,)), dma((12,)), dma((12,)),
            dma((groups,)), dma((groups,)),
            dma((12,)), dma((12,)), dma((12,)), dma((12,)),
            dma((3 * PASSES,)), dma((3 * PASSES,)),
            dma((groups,)), dma((groups,)), dma((12,)), dma((12,)), dma((groups,)), dma((groups,)),
        ],
        compiler_params=pltpu.CompilerParams(
            collective_id=0, has_side_effects=True, vmem_limit_bytes=60 * 1024 * 1024
        ),
        cost_estimate=pl.CostEstimate(
            flops=5 * 2 * slots * width * hid, bytes_accessed=26_000_000, transcendentals=slots * hid
        ),
    )(send, w_gate, w_up, w_down)

    steps = half // NB
    columns = quarter // steps
    return pl.pallas_call(
        finish_kernel,
        grid=(steps,),
        out_shape=(
            jax.ShapeDtypeStruct(tokens.shape, bf16),
            jax.ShapeDtypeStruct((quarter, hid), bf16),
            jax.ShapeDtypeStruct((quarter, hid), bf16),
            jax.ShapeDtypeStruct((hid, quarter), bf16),
        ),
        in_specs=[
            pl.BlockSpec((DP * BLOCKS, ROW, columns), lambda i: (0, 0, i)),
            pl.BlockSpec((DP, slots, 3 * hid), lambda i: (0, 0, 0)),
            pl.BlockSpec((EXPERTS, ROW, NB), lambda i: (0, 0, i)),
            pl.BlockSpec((tokens.shape[0], EXPERTS * CAP), lambda i: (0, 0)),
        ],
        out_specs=(
            pl.BlockSpec((tokens.shape[0], 2 * NB), lambda i: (0, i)),
            pl.BlockSpec((columns, hid), lambda i: (i, 0)),
            pl.BlockSpec((columns, hid), lambda i: (i, 0)),
            pl.BlockSpec((hid, columns), lambda i: (0, i)),
        ),
        scratch_shapes=[pltpu.VMEM((hid, DP * slots), bf16)],
        compiler_params=pltpu.CompilerParams(vmem_limit_bytes=60 * 1024 * 1024),
        cost_estimate=pl.CostEstimate(
            flops=3 * 2 * slots * width * hid, bytes_accessed=18_000_000, transcendentals=0
        ),
    )(xbuf.reshape(DP * BLOCKS, ROW, quarter), dall, fin, pick)


def solution(mesh):
    in_specs = (
        P(("dp", "expert"), None),
        P(("dp", "expert"), None),
        P(("dp", "expert"), None),
        P(("dp", "expert"), None),
        P(None, "expert"),
        P(None, "expert"),
        P("expert", None),
    )
    out_specs = (P(("dp", "expert"), None), P("dp", "expert"), P("dp", "expert"), P("expert", "dp"))
    return jax.shard_map(body, mesh=mesh, in_specs=in_specs, out_specs=out_specs, check_vma=False)
```

time: 314 us -> 106 us (0.34)
  waiting for transfers between devices: 176 us -> 0 us
  Pallas kernels: 0 us -> 99.2 us
  blocking collectives: 51.9 us -> 0 us
  matrix products: 47.8 us -> 0.78 us
  starting transfers between devices: 16.9 us -> 0 us
  between operations: 13.9 us -> 0.71 us
  local copies, waits for them, and re-layouts: 4.95 us -> 0.8 us
    pallas_call x0 -> x2, Pallas kernels: none -> 99.2 us  [the longest x1 88.2 us: body(): pl.pallas_call(exchange_kernel, out_shape=(jax.ShapeDtypeStruct((DP, BLOC...]
    reduce_scatter x3 -> x0, waiting for transfers between devices: 97.8 us -> none  [the longest x1 60.3 us: body(): lax.psum_scatter(g_gate.astype(jnp.bfloat16), 'dp', scatter_dimension=0,...]
    all_to_all x2 -> x0, waiting for transfers between devices: 78.4 us -> none  [the longest x1 43.9 us: body(): lax.all_to_all(send_in, 'expert', split_axis=0, concat_axis=0, tiled=True)]
    all_to_all x1 -> x0, blocking collectives: 51.9 us -> none  [body(): lax.all_to_all(back.reshape(peer_count, CAP, width).astype(jnp.bfloat16),...]
    dot_general x9 -> x0, matrix products: 45.6 us -> none  [the longest x1 6.6 us: weight_terms(): lax.dot_general(rows_in, d_gate, contract_rows, preferred_element_type=jn...]
    all_to_all x2 -> x0, starting transfers between devices: 16.6 us -> none  [the longest x1 9.78 us: body(): lax.all_to_all(send_in, 'expert', split_axis=0, concat_axis=0, tiled=True)]
    broadcast_in_dim x2 -> x0, local copies, waits for them, and re-layouts: 4.48 us -> none  [the longest x1 2.24 us: body(): jnp.broadcast_to(slot_inputs[:, None], (experts, SPLIT, CAP, width))]
  transfers between devices with their start and end apart: 5 -> 0, of which waited for: 4 -> 0; matrix products, arithmetic and copies ran while one was open for 13% -> 0% of each run, Pallas kernels for 0% -> 0%
where the time goes in v2:
time: 106 us; the launch traced here: 105 us
  Pallas kernels  99.2 us (94%)
  other arithmetic  3.91 us (4%)
    pallas_call x1, Pallas kernels, body(): pl.pallas_call(exchange_kernel, out_shape=(jax.ShapeDtypeStruct((DP, BLOC...  88.2 us
    pallas_call x1, Pallas kernels, body(): pl.pallas_call(finish_kernel, grid=(steps,), out_shape=(jax.ShapeDtypeStr...  11 us

profile of v2, /device:TPU:1, one launch (start us, length us, event | category | flops | bytes accessed | tf_op | source)
XLA Modules:
  0.0 105.4 jit_solution(10199836763584908959)
XLA Ops:
  0.6 0.0 copy-start
  0.6 0.8 convert_reduce_fusion
  1.5 0.3 reduce_window_sum.11
  1.8 0.1 eq.67
  1.9 0.8 fusion.18
  2.7 0.1 copy.17
  2.8 0.1 copy.15
  2.9 0.0 copy-start.1
  2.9 0.6 and_convert_fusion.pick
  3.6 0.0 copy-done
  3.6 0.4 fusion.1
  4.0 0.5 copy-done.1
  4.4 0.4 convolution_convert_fusion
  4.8 1.4 %pad_maximum_fusion.send = bf16[8,16,7168]{2,1,0:T(8,128)(2,1)} fusion(bf16[8,8,7168]{2,1,0:T(8,128)(2,1)S(1)} %fusion.1, bf16[8,8,7168]{2,1,0:T(8,128)(2,1)S(1)} %convolution_convert_fusion), kind=kLoop, calls=%fused_computation.4 | loop fusion | flops 3670016 | bytes 3670016 | tf_op jit(solution)/shard_map/concatenate | solution.py:359
  6.2 88.2 %shard_map.102 = (bf16[4,32,16,1792]{3,2,1,0:T(8,128)(2,1)}, bf16[4,256,1152]{2,1,0:T(8,128)(2,1)}, bf16[8,16,3584]{2,1,0:T(8,128)(2,1)}) custom-call(bf16[8,16,7168]{2,1,0:T(8,128)(2,1)} %pad_maximum_fusion.send, bf16[7168,384]{1,0:T(8,128)(2,1)} %wg.1, bf16[7168,384]{1,0:T(8,128)(2,1)} %wu.1, bf16[384,7168]{1,0:T(8,128)(2,1)} %wd.1), custom_call_target="tpu_custom_call" | custom-call | flops 7046430720 | bytes 26000000 | tf_op jit(solution)/shard_map/pallas_call | solution.py:365
  94.4 11.0 %shard_map.103 = (bf16[128,7168]{1,0:T(8,128)(2,1)}, bf16[1792,384]{1,0:T(8,128)(2,1)}, bf16[1792,384]{1,0:T(8,128)(2,1)}, bf16[384,1792]{1,0:T(8,128)(2,1)}) custom-call(bf16[128,16,1792]{2,1,0:T(8,128)(2,1)} %bitcast.15, bf16[4,256,1152]{2,1,0:T(8,128)(2,1)} %get-tuple-element.8.dall, bf16[8,16,3584]{2,1,0:T(8,128)(2,1)} %get-tuple-element.9.fin, ...), custom_call_target="tpu_custom_call" | custom-call | flops 4227858432 | bytes 18000000 | tf_op jit(solution)/shard_map/pallas_call | solution.py:403
  (6 shorter events, 0.0 us)
Async XLA Ops:
  0.6 2.9 %copy-start = (bf16[128,7168]{1,0:T(8,128)(2,1)S(1)}, bf16[128,7168]{1,0:T(8,128)(2,1)}, u32[]{:S(2)}) copy-start(bf16[128,7168]{1,0:T(8,128)(2,1)} %param.8) | copy-start | bytes 5505028
  2.9 1.5 %copy-start.1 = (bf16[128,7168]{1,0:T(8,128)(2,1)S(1)}, bf16[128,7168]{1,0:T(8,128)(2,1)}, u32[]{:S(2)}) copy-start(bf16[128,7168]{1,0:T(8,128)(2,1)} %param.7) | copy-start | bytes 5505028

commit v3 on v2

--- a/solution.py
+++ b/solution.py
@@ -11,8 +11,7 @@
 EXPERTS = 8
 BLOCKS = 32
 DY = (0, 1, 3, 2)
-PASSES = 2
-PER_PASS = len(DY) // PASSES
+PASSES = ((0, 1), (2,), (3,))
 KCH = 1024
 NB = 512
 MESH = pl.DeviceIdType.MESH
@@ -24,10 +23,10 @@
 
 
 def exchange_kernel(
-    send, wg, wu, wd,
-    xbuf, dall, fin,
-    recv, mid, wgu, wdv, dloc, gu_acc, dh_acc, ret, sib, zin, zsum,
-    w_sem, own_sem, keep_sem, dk_sem, fk_sem,
+    tokens, grad_out, ids, weights, wg, wu, wd,
+    xbuf, dall, fin, pick,
+    tok, grad, send, recv, mid, wgu, wdv, dloc, ret, sib, zin, zsum,
+    t_sem, w_sem, own_sem, keep_sem, dk_sem, fk_sem,
     ys_sem, yr_sem, zs_sem, zr_sem, fs_sem, fr_sem, xs_sem, xr_sem, xfs_sem, xfr_sem,
     gs_sem, gr_sem, ss_sem, sr_sem, rs_sem, rr_sem, bs_sem, br_sem,
 ):
@@ -58,9 +57,51 @@
     sources = [lax.rem(x - d + DP, DP) for d in range(1, DP)]
 
     barrier = pltpu.get_barrier_semaphore()
-    near = [device(ahead[g], z, k) for g in (1, 2, 3)] + [device(y, t, k) for t in zs]
-    for to in near + peers + [sibling]:
+    around = [device(ahead[g], z, k) for g in (1, 2, 3)] + [device(y, t, k) for t in zs]
+    for to in around + peers + [sibling]:
         pl.semaphore_signal(barrier, inc=1, device_id=to, device_id_type=MESH)
+
+    fetch = [
+        pltpu.make_async_copy(tokens, tok, t_sem.at[0]),
+        pltpu.make_async_copy(grad_out, grad, t_sem.at[1]),
+    ]
+    for copy in fetch:
+        copy.start()
+    count = tok.shape[0]
+    topk = ids.shape[0]
+    slots = EXPERTS * CAP
+    ids_t = ids[...].astype(jnp.float32)
+    weights_t = weights[...]
+    wanted = lax.broadcasted_iota(jnp.int32, (EXPERTS, topk, count), 0).astype(jnp.float32)
+    chosen = ids_t[None] == wanted
+    member = jnp.sum(jnp.where(chosen, 1.0, 0.0), axis=1)
+    weight = jnp.sum(jnp.where(chosen, weights_t[None], 0.0), axis=1)
+    upto = lax.broadcasted_iota(jnp.int32, (count, count), 0) <= lax.broadcasted_iota(
+        jnp.int32, (count, count), 1
+    )
+    position = jnp.dot(
+        member.astype(jnp.bfloat16), jnp.where(upto, 1.0, 0.0).astype(jnp.bfloat16),
+        preferred_element_type=jnp.float32,
+    )
+    place = lax.broadcasted_iota(jnp.int32, (EXPERTS, CAP, count), 1).astype(jnp.float32) + 1.0
+    held = jnp.where((position[:, None, :] == place) & (member[:, None, :] == 1.0), 1.0, 0.0)
+    slot_gate = jnp.sum(held * weight[:, None, :], axis=2, keepdims=True).reshape(slots, 1)
+    picker = held.reshape(slots, count).astype(jnp.bfloat16)
+    pick[...] = picker
+    for copy in fetch:
+        copy.wait()
+
+    def fill(i, carry):
+        at = pl.ds(pl.multiple_of(i * KCH, KCH), KCH)
+        slot_inputs = jnp.dot(picker, tok[:, at], preferred_element_type=jnp.float32)
+        raw_grads = jnp.dot(picker, grad[:, at], preferred_element_type=jnp.float32)
+        send[:, pl.ds(0, CAP), at] = slot_inputs.reshape(EXPERTS, CAP, KCH).astype(jnp.bfloat16)
+        send[:, pl.ds(CAP, CAP), at] = (
+            (slot_gate * raw_grads).reshape(EXPERTS, CAP, KCH).astype(jnp.bfloat16)
+        )
+        return carry
+
+    lax.fori_loop(0, width // KCH, fill, 0)
     pl.semaphore_wait(barrier, 10)
 
     def own_block(g, zz):
@@ -108,41 +149,52 @@
             xs_sem.at[g * 3 + d], xr_sem.at[g * 3 + d], peers[d],
         )
 
+    def exchange_block(g, d, zz):
+        to = peers[d][0]
+        columns = pl.ds(pl.multiple_of(to * quarter, 128), quarter)
+        at = own_block(g, zz)
+        return remote(
+            recv.at[at, :, columns], xbuf.at[x, at],
+            xs_sem.at[g * 3 + d], xr_sem.at[g * 3 + d], peers[d],
+        )
+
     def exchange_forward(g, d):
         at = xbuf.at[sources[d], pl.ds(own_block(g, 0), 4)]
         return remote(at, at, xfs_sem.at[g * 3 + d], xfr_sem.at[g * 3 + d], sibling)
 
+    def blocks_of(p):
+        return pl.ds(PASSES[p][0] * 8, len(PASSES[p]) * 8)
+
+    def rows_of(p):
+        return pl.ds(PASSES[p][0] * 8 * CAP, len(PASSES[p]) * 8 * CAP)
+
     def keep(p):
-        at = pl.ds(p * 8 * PER_PASS, 8 * PER_PASS)
+        at = blocks_of(p)
         columns = pl.ds(pl.multiple_of(x * quarter, 128), quarter)
         return pltpu.make_async_copy(recv.at[at, :, columns], xbuf.at[x, at], keep_sem.at[p])
 
-    rows = PER_PASS * 8 * CAP
-
     def gather(p, d):
-        at = pl.ds(p * rows, rows)
+        at = rows_of(p)
         return remote(
             dloc.at[at], dall.at[x, at], gs_sem.at[p * 3 + d], gr_sem.at[p * 3 + d], peers[d]
         )
 
     def keep_terms(p):
-        at = pl.ds(p * rows, rows)
+        at = rows_of(p)
         return pltpu.make_async_copy(dloc.at[at], dall.at[x, at], dk_sem.at[p])
 
-    def relay(g):
-        for far in (0, 1):
-            along_y(g, far).wait_recv()
-        for t in range(3):
-            along_z(g, t).start()
-
-    def arrive(g):
+    def near(g):
         if g == 0:
             own.wait()
-        for t in range(3):
-            z_arrival(g, t).wait_recv()
-        forward(g).start()
-        for d in range(3):
-            exchange(g, d).start()
+        else:
+            along_y(g, 0).wait_recv()
+        for d in range(3):
+            exchange_block(g, d, z).start()
+
+    def arrive(g, t):
+        z_arrival(g, t).wait_recv()
+        for d in range(3):
+            exchange_block(g, d, zs[t]).start()
 
     def exchanged(g):
         for d in range(3):
@@ -150,32 +202,28 @@
             exchange_forward(g, d).start()
 
     def terms(p):
-        for g in range(p * PER_PASS, (p + 1) * PER_PASS):
+        for g in PASSES[p]:
             forward(g).wait_recv()
         keep(p).start()
-        blocks = pl.ds(p * 8 * PER_PASS, 8 * PER_PASS)
-        gu_acc[...] = jnp.zeros_like(gu_acc)
-        dh_acc[...] = jnp.zeros_like(dh_acc)
-
-        def contract(i, carry):
-            at = pl.ds(pl.multiple_of(i * KCH, KCH), KCH)
-            gu_acc[...] += jnp.dot(
+        blocks = blocks_of(p)
+        size = len(PASSES[p]) * 8 * CAP
+        both = jnp.zeros((size, 2 * hid), jnp.float32)
+        d_hidden = jnp.zeros((size, hid), jnp.float32)
+        for i in range(width // KCH):
+            at = pl.ds(i * KCH, KCH)
+            both += jnp.dot(
                 flat(recv[blocks, pl.ds(0, CAP), at]), wgu[at, :],
                 preferred_element_type=jnp.float32,
             )
-            dh_acc[...] += lax.dot_general(
+            d_hidden += lax.dot_general(
                 flat(recv[blocks, pl.ds(CAP, CAP), at]), wdv[:, at],
                 (((1,), (1,)), ((), ())), preferred_element_type=jnp.float32,
             )
-            return carry
-
-        lax.fori_loop(0, width // KCH, contract, 0)
-        gate_pre = gu_acc[:, :hid]
-        up_pre = gu_acc[:, hid:]
-        d_hidden = dh_acc[...]
+        gate_pre = both[:, :hid]
+        up_pre = both[:, hid:]
         sig = jax.nn.sigmoid(gate_pre)
         act = gate_pre * sig
-        at = pl.ds(p * rows, rows)
+        at = rows_of(p)
         dloc[at, pl.ds(0, hid)] = (
             d_hidden * up_pre * sig * (1.0 + gate_pre * (1.0 - sig))
         ).astype(jnp.bfloat16)
@@ -195,19 +243,19 @@
         def columns(b, carry):
             for h in range(2):
                 out = lax.dot_general(
-                    dloc[pl.ds(p * rows, rows), pl.ds(0, 2 * hid)],
+                    dloc[rows_of(p), pl.ds(0, 2 * hid)],
                     wgu[pl.ds(pl.multiple_of(b * 2 * NB + h * NB, NB), NB), :],
                     (((1,), (1,)), ((), ())),
                     preferred_element_type=jnp.float32,
                 )
                 ret[
-                    pl.ds(p * 8 * PER_PASS, 8 * PER_PASS), pl.ds(h * CAP, CAP),
+                    blocks_of(p), pl.ds(h * CAP, CAP),
                     pl.ds(pl.multiple_of(b * NB, NB), NB),
-                ] = out.reshape(8 * PER_PASS, CAP, NB).astype(jnp.bfloat16)
+                ] = out.reshape(8 * len(PASSES[p]), CAP, NB).astype(jnp.bfloat16)
             return carry
 
         lax.fori_loop(0, width // (2 * NB), columns, 0)
-        for g in range(p * PER_PASS, (p + 1) * PER_PASS):
+        for g in PASSES[p]:
             to_sibling(g).start()
 
     def return_z(g, t):
@@ -224,7 +272,7 @@
         return (a.astype(jnp.float32) + b.astype(jnp.float32)).astype(jnp.bfloat16)
 
     def give_back(p):
-        for g in range(p * PER_PASS, (p + 1) * PER_PASS):
+        for g in PASSES[p]:
             to_sibling(g).wait_recv()
 
             def add(i, carry, g=g):
@@ -246,7 +294,7 @@
     home = pltpu.make_async_copy(zsum.at[pl.ds(0, 2)], fin.at[pl.ds(2 * y, 2)], fk_sem)
 
     def relay_back(p):
-        for g in range(p * PER_PASS, (p + 1) * PER_PASS):
+        for g in PASSES[p]:
             for t in range(3):
                 return_arrival(g, t).wait_recv()
 
@@ -263,39 +311,67 @@
     own.start()
     for t in range(3):
         along_z(0, t).start()
-    for g in (1, 2):
-        for far in (0, 1):
+    for far in (0, 1):
+        for g in (1, 2):
             along_y(g, far).start()
     for load in loads:
         load.start()
-    relay(1)
+    near(0)
+    near(1)
+    along_z(1, 0).start()
+    near(2)
+    for g in (1, 2):
+        along_y(g, 1).wait_recv()
     for far in (0, 1):
         along_y(3, far).start()
-    arrive(0)
-    relay(2)
-    arrive(1)
-    relay(3)
     for load in loads:
         load.wait()
+    arrive(0, 0)
+    along_z(1, 1).start()
+    arrive(0, 1)
+    along_z(1, 2).start()
+    arrive(0, 2)
+    along_z(2, 0).start()
+    forward(0).start()
+    arrive(1, 0)
+    along_z(2, 1).start()
+    arrive(1, 1)
+    along_z(2, 2).start()
+    near(3)
+    along_y(3, 1).wait_recv()
+    arrive(1, 2)
+    along_z(3, 0).start()
+    forward(1).start()
     terms(0)
+    arrive(2, 0)
+    along_z(3, 1).start()
+    arrive(2, 1)
+    along_z(3, 2).start()
     back(0)
-    arrive(2)
+    arrive(2, 2)
+    forward(2).start()
     exchanged(0)
-    arrive(3)
+    terms(1)
+    give_back(0)
+    back(1)
     exchanged(1)
-    give_back(0)
-    terms(1)
+    for t in range(3):
+        arrive(3, t)
+    forward(3).start()
+    give_back(1)
+    terms(2)
+    back(2)
+    give_back(2)
     relay_back(0)
-    back(1)
     exchanged(2)
-    give_back(1)
+    relay_back(1)
     exchanged(3)
-    relay_back(1)
+    relay_back(2)
 
     for g in range(4):
         for d in range(3):
             exchange_forward(g, d).wait_recv()
-    for p in range(PASSES):
+    for p in range(len(PASSES)):
         keep(p).wait()
         keep_terms(p).wait()
         for d in range(3):
@@ -324,8 +400,9 @@
     def _():
         hid_t[...] = dall[:, :, 2 * hid:].reshape(rows, hid).T
 
-    rows_in = flat(xbuf[:, pl.ds(0, CAP), :])
-    rows_grad = flat(xbuf[:, pl.ds(CAP, CAP), :])
+    blocks = xbuf.shape[0] * xbuf.shape[1]
+    rows_in = flat(xbuf[:, :, pl.ds(0, CAP), :].reshape(blocks, CAP, xbuf.shape[3]))
+    rows_grad = flat(xbuf[:, :, pl.ds(CAP, CAP), :].reshape(blocks, CAP, xbuf.shape[3]))
     out = jnp.dot(
         rows_in.T, dall[:, :, : 2 * hid].reshape(rows, 2 * hid), preferred_element_type=jnp.float32
     )
@@ -334,7 +411,7 @@
     gd[...] = jnp.dot(hid_t[...], rows_grad, preferred_element_type=jnp.float32).astype(jnp.bfloat16)
     for h in range(2):
         gt[:, pl.ds(h * NB, NB)] = jnp.dot(
-            pick[...], flat(fin[:, pl.ds(h * CAP, CAP), :]), preferred_element_type=jnp.float32
+            pick[...].T, flat(fin[:, pl.ds(h * CAP, CAP), :]), preferred_element_type=jnp.float32
         ).astype(jnp.bfloat16)
 
 
@@ -344,59 +421,49 @@
     half = width // 2
     quarter = width // DP
     slots = BLOCKS * CAP
-    chosen = expert_ids[None, :, :] == jnp.arange(EXPERTS, dtype=jnp.int32)[:, None, None]
-    member = jnp.sum(chosen.astype(jnp.int32), axis=2)
-    weight = jnp.sum(jnp.where(chosen, gate_weights[None, :, :], jnp.float32(0.0)), axis=2)
-    position = jnp.cumsum(member, axis=1) - 1
-    slot_mask = (member[..., None] == 1) & (position[..., None] == jnp.arange(CAP, dtype=jnp.int32))
-    picker = slot_mask.astype(jnp.bfloat16)
-    slot_inputs = jnp.einsum(
-        "etc,td->ecd", picker, tokens, preferred_element_type=jnp.float32
-    ).astype(jnp.bfloat16)
-    raw_grads = jnp.einsum("etc,td->ecd", picker, grad_out, preferred_element_type=jnp.float32)
-    slot_gate = jnp.sum(slot_mask.astype(jnp.float32) * weight[..., None], axis=1)
-    slot_grads = (slot_gate[..., None] * raw_grads).astype(jnp.bfloat16)
-    send = jnp.concatenate([slot_inputs, slot_grads], axis=1)
-    pick = jnp.transpose(picker, (1, 0, 2)).reshape(tokens.shape[0], EXPERTS * CAP)
     any_spec = pl.BlockSpec(memory_space=pl.ANY)
+    vmem = pl.BlockSpec(memory_space=pltpu.VMEM)
     bf16 = jnp.bfloat16
     dma = pltpu.SemaphoreType.DMA
     groups = len(DY)
-    xbuf, dall, fin = pl.pallas_call(
+    passes = len(PASSES)
+    xbuf, dall, fin, pick = pl.pallas_call(
         exchange_kernel,
         out_shape=(
-            jax.ShapeDtypeStruct((DP, BLOCKS, ROW, quarter), bf16),
-            jax.ShapeDtypeStruct((DP, slots, 3 * hid), bf16),
-            jax.ShapeDtypeStruct((EXPERTS, ROW, half), bf16),
+            pltpu.VMEM((DP, BLOCKS, ROW, quarter), bf16),
+            pltpu.VMEM((DP, slots, 3 * hid), bf16),
+            pltpu.VMEM((EXPERTS, ROW, half), bf16),
+            jax.ShapeDtypeStruct((EXPERTS * CAP, tokens.shape[0]), bf16),
         ),
-        in_specs=[any_spec] * 4,
-        out_specs=(any_spec,) * 3,
+        in_specs=[any_spec] * 2 + [vmem] * 2 + [any_spec] * 3,
+        out_specs=(any_spec,) * 3 + (vmem,),
         scratch_shapes=[
+            pltpu.VMEM(tokens.shape, bf16),
+            pltpu.VMEM(tokens.shape, bf16),
+            pltpu.VMEM((EXPERTS, ROW, width), bf16),
             pltpu.VMEM((BLOCKS, ROW, width), bf16),
             pltpu.VMEM((3, ROW, width), bf16),
             pltpu.VMEM((width, 2 * hid), bf16),
             pltpu.VMEM((hid, width), bf16),
             pltpu.VMEM((slots, 3 * hid), bf16),
-            pltpu.VMEM((slots // PASSES, 2 * hid), jnp.float32),
-            pltpu.VMEM((slots // PASSES, hid), jnp.float32),
             pltpu.VMEM((BLOCKS, ROW, half), bf16),
             pltpu.VMEM((BLOCKS // 2, ROW, half), bf16),
             pltpu.VMEM((BLOCKS // 2, ROW, half), bf16),
             pltpu.VMEM((EXPERTS, ROW, half), bf16),
-            dma((3,)), dma, dma((PASSES,)), dma((PASSES,)), dma,
+            dma((2,)), dma((3,)), dma, dma((passes,)), dma((passes,)), dma,
             dma((8,)), dma((8,)), dma((12,)), dma((12,)),
             dma((groups,)), dma((groups,)),
             dma((12,)), dma((12,)), dma((12,)), dma((12,)),
-            dma((3 * PASSES,)), dma((3 * PASSES,)),
+            dma((3 * passes,)), dma((3 * passes,)),
             dma((groups,)), dma((groups,)), dma((12,)), dma((12,)), dma((groups,)), dma((groups,)),
         ],
         compiler_params=pltpu.CompilerParams(
-            collective_id=0, has_side_effects=True, vmem_limit_bytes=60 * 1024 * 1024
+            collective_id=0, has_side_effects=True, vmem_limit_bytes=44 * 1024 * 1024
         ),
         cost_estimate=pl.CostEstimate(
             flops=5 * 2 * slots * width * hid, bytes_accessed=26_000_000, transcendentals=slots * hid
         ),
-    )(send, w_gate, w_up, w_down)
+    )(tokens, grad_out, expert_ids.T, gate_weights.T, w_gate, w_up, w_down)
 
     steps = half // NB
     columns = quarter // steps
@@ -410,10 +477,10 @@
             jax.ShapeDtypeStruct((hid, quarter), bf16),
         ),
         in_specs=[
-            pl.BlockSpec((DP * BLOCKS, ROW, columns), lambda i: (0, 0, i)),
+            pl.BlockSpec((DP, BLOCKS, ROW, columns), lambda i: (0, 0, 0, i)),
             pl.BlockSpec((DP, slots, 3 * hid), lambda i: (0, 0, 0)),
             pl.BlockSpec((EXPERTS, ROW, NB), lambda i: (0, 0, i)),
-            pl.BlockSpec((tokens.shape[0], EXPERTS * CAP), lambda i: (0, 0)),
+            pl.BlockSpec((EXPERTS * CAP, tokens.shape[0]), lambda i: (0, 0)),
         ],
         out_specs=(
             pl.BlockSpec((tokens.shape[0], 2 * NB), lambda i: (0, i)),
@@ -422,11 +489,11 @@
             pl.BlockSpec((hid, columns), lambda i: (0, i)),
         ),
         scratch_shapes=[pltpu.VMEM((hid, DP * slots), bf16)],
-        compiler_params=pltpu.CompilerParams(vmem_limit_bytes=60 * 1024 * 1024),
+        compiler_params=pltpu.CompilerParams(vmem_limit_bytes=20 * 1024 * 1024),
         cost_estimate=pl.CostEstimate(
             flops=3 * 2 * slots * width * hid, bytes_accessed=18_000_000, transcendentals=0
         ),
-    )(xbuf.reshape(DP * BLOCKS, ROW, quarter), dall, fin, pick)
+    )(xbuf, dall, fin, pick)
 
 
 def solution(mesh):

time: 106 us -> 97.4 us (0.919)
  other arithmetic: 3.91 us -> 0 us
  Pallas kernels: 99.2 us -> 95.8 us
    pallas_call x1, Pallas kernels: 11 us -> 7.89 us  [body(): pl.pallas_call(finish_kernel, grid=(steps,), out_shape=(jax.ShapeDtypeStr...]
    concatenate x1 -> x0, other arithmetic: 1.35 us -> none  [body(): send = jnp.concatenate([slot_inputs, slot_grads], axis=1)]
where the time goes in v3:
time: 97.4 us; the launch traced here: 97.2 us
  Pallas kernels  95.8 us (98%)
    pallas_call x1, Pallas kernels, body(): pl.pallas_call(exchange_kernel, out_shape=(pltpu.VMEM((DP, BLOCKS, ROW, q...  87.9 us
    pallas_call x1, Pallas kernels, body(): pl.pallas_call(finish_kernel, grid=(steps,), out_shape=(jax.ShapeDtypeStr...  7.89 us

profile of v3, /device:TPU:1, one launch (start us, length us, event | category | flops | bytes accessed | tf_op | source)
XLA Modules:
  0.0 97.2 jit_solution(15078936927028336016)
XLA Ops:
  0.6 87.9 %shard_map.102 = (bf16[4,32,16,1792]{3,2,1,0:T(8,128)(2,1)S(1)}, bf16[4,256,1152]{2,1,0:T(8,128)(2,1)S(1)}, bf16[8,16,3584]{2,1,0:T(8,128)(2,1)S(1)}, bf16[64,128]{1,0:T(8,128)(2,1)}) custom-call(bf16[128,7168]{1,0:T(8,128)(2,1)} %tokens.1, bf16[128,7168]{1,0:T(8,128)(2,1)} %grad_out.1, s32[8,128]{1,0:T(8,128)} %bitcast.2, f32[8,128]{1,0:T(8,128)} %bitcast.3, ...), custom_call_target="tpu_custom_call" | custom-call | flops 7046430720 | bytes 26000000 | tf_op jit(solution)/shard_map/pallas_call | solution.py:430
  88.5 0.0 copy-start
  88.6 0.7 copy-done
  89.3 7.9 %shard_map.103 = (bf16[128,7168]{1,0:T(8,128)(2,1)}, bf16[1792,384]{1,0:T(8,128)(2,1)}, bf16[1792,384]{1,0:T(8,128)(2,1)}, bf16[384,1792]{1,0:T(8,128)(2,1)}) custom-call(bf16[4,32,16,1792]{3,2,1,0:T(8,128)(2,1)S(1)} %get-tuple-element.8.xbuf, bf16[4,256,1152]{2,1,0:T(8,128)(2,1)S(1)} %get-tuple-element.9.dall, ...), custom_call_target="tpu_custom_call" | custom-call | flops 4227858432 | bytes 18000000 | tf_op jit(solution)/shard_map/pallas_call | solution.py:470
Async XLA Ops:
  88.5 0.7 copy-start

commit v4 on v3

--- a/solution.py
+++ b/solution.py
@@ -11,10 +11,12 @@
 EXPERTS = 8
 BLOCKS = 32
 DY = (0, 1, 3, 2)
-PASSES = ((0, 1), (2,), (3,))
+PASSES = ((0, 1), (2, 3))
 KCH = 1024
 NB = 512
 MESH = pl.DeviceIdType.MESH
+RELAYED = (True, False)
+PARTS = (((0, 7),), ((0, 4), (4, 3)))
 
 
 def flat(block):
@@ -173,11 +175,34 @@
         columns = pl.ds(pl.multiple_of(x * quarter, 128), quarter)
         return pltpu.make_async_copy(recv.at[at, :, columns], xbuf.at[x, at], keep_sem.at[p])
 
-    def gather(p, d):
+    right, left = peers[0], peers[2]
+    before, after = sources[0], sources[2]
+
+    def gather(p, side):
         at = rows_of(p)
         return remote(
-            dloc.at[at], dall.at[x, at], gs_sem.at[p * 3 + d], gr_sem.at[p * 3 + d], peers[d]
-        )
+            dloc.at[at], dall.at[x, at], gs_sem.at[p * 4 + side], gr_sem.at[p * 4 + side],
+            left if side else right,
+        )
+
+    def gather_far(p):
+        at = rows_of(p)
+        return remote(
+            dloc.at[at], dall.at[x, at], gs_sem.at[p * 4 + 2], gr_sem.at[p * 4 + 2], peers[1]
+        )
+
+    def hand_on(p, side):
+        size = len(PASSES[p]) * 4 * CAP
+        at = dall.at[after if side else before, pl.ds(PASSES[p][0] * 8 * CAP + side * size, size)]
+        return remote(
+            at, at, gs_sem.at[p * 4 + 2 + side], gr_sem.at[p * 4 + 2 + side],
+            left if side else right,
+        )
+
+    def spread(p):
+        for side in (0, 1):
+            gather(p, side).wait_recv()
+            hand_on(p, side).start()
 
     def keep_terms(p):
         at = rows_of(p)
@@ -229,18 +254,28 @@
         ).astype(jnp.bfloat16)
         dloc[at, pl.ds(hid, hid)] = (d_hidden * act).astype(jnp.bfloat16)
         dloc[at, pl.ds(2 * hid, hid)] = (act * up_pre).astype(jnp.bfloat16)
-        for d in range(3):
-            gather(p, d).start()
+        for side in (0, 1):
+            gather(p, side).start()
+        if not RELAYED[p]:
+            gather_far(p).start()
         keep_terms(p).start()
 
-    def to_sibling(g):
-        return remote(
-            ret.at[pl.ds(g * 8 + (1 - k) * 4, 4)], sib.at[pl.ds(g * 4, 4)],
-            ss_sem.at[g], sr_sem.at[g], sibling,
-        )
-
-    def back(p):
-        def columns(b, carry):
+    def part_of(g, part):
+        first, size = next(PARTS[p] for p in range(len(PASSES)) if g in PASSES[p])[part]
+        return pl.ds(first * NB, size * NB)
+
+    def to_sibling(g, part):
+        at = part_of(g, part)
+        return remote(
+            ret.at[pl.ds(g * 8 + (1 - k) * 4, 4), :, at], sib.at[pl.ds(g * 4, 4), :, at],
+            ss_sem.at[g * 2 + part], sr_sem.at[g * 2 + part], sibling,
+        )
+
+    def back(p, part):
+        first, size = PARTS[p][part]
+
+        def columns(i, carry):
+            b = first + i
             for h in range(2):
                 out = lax.dot_general(
                     dloc[rows_of(p), pl.ds(0, 2 * hid)],
@@ -249,64 +284,73 @@
                     preferred_element_type=jnp.float32,
                 )
                 ret[
-                    blocks_of(p), pl.ds(h * CAP, CAP),
-                    pl.ds(pl.multiple_of(b * NB, NB), NB),
+                    blocks_of(p), pl.ds(h * CAP, CAP), pl.ds(pl.multiple_of(b * NB, NB), NB)
                 ] = out.reshape(8 * len(PASSES[p]), CAP, NB).astype(jnp.bfloat16)
             return carry
 
-        lax.fori_loop(0, width // (2 * NB), columns, 0)
+        lax.fori_loop(0, size, columns, 0, unroll=True)
         for g in PASSES[p]:
-            to_sibling(g).start()
-
-    def return_z(g, t):
-        return remote(
-            ret.at[own_block(g, zs[t])], zin.at[g * 4 + z],
-            rs_sem.at[g * 3 + t], rr_sem.at[g * 3 + t], device(y, zs[t], k),
-        )
-
-    def return_arrival(g, t):
-        at = zin.at[g * 4 + zs[t]]
-        return remote(at, at, rs_sem.at[g * 3 + t], rr_sem.at[g * 3 + t], device(y, zs[t], k))
+            to_sibling(g, part).start()
+
+    def return_z(g, t, part):
+        at = part_of(g, part)
+        return remote(
+            ret.at[own_block(g, zs[t]), :, at], zin.at[g * 4 + z, :, at],
+            rs_sem.at[(g * 3 + t) * 2 + part], rr_sem.at[(g * 3 + t) * 2 + part],
+            device(y, zs[t], k),
+        )
+
+    def return_arrival(g, t, part):
+        at = zin.at[g * 4 + zs[t], :, part_of(g, part)]
+        return remote(
+            at, at, rs_sem.at[(g * 3 + t) * 2 + part], rr_sem.at[(g * 3 + t) * 2 + part],
+            device(y, zs[t], k),
+        )
 
     def plus(a, b):
         return (a.astype(jnp.float32) + b.astype(jnp.float32)).astype(jnp.bfloat16)
 
-    def give_back(p):
+    def give_back(p, part):
         for g in PASSES[p]:
-            to_sibling(g).wait_recv()
-
-            def add(i, carry, g=g):
+            to_sibling(g, part).wait_recv()
+            columns = part_of(g, part)
+
+            def add(i, carry, g=g, columns=columns):
                 at = own_block(g, i)
-                ret[at] = plus(ret[at], sib[g * 4 + i])
+                ret[at, :, columns] = plus(ret[at, :, columns], sib[g * 4 + i, :, columns])
                 return carry
 
             lax.fori_loop(0, 4, add, 0)
             for t in range(3):
-                return_z(g, t).start()
-            zin[g * 4 + z] = ret[own_block(g, z)]
-
-    def return_y(g):
-        return remote(
-            zsum.at[pl.ds(2 * g, 2)], fin.at[pl.ds(2 * y, 2)],
-            bs_sem.at[g], br_sem.at[g], device(behind[g], z, k),
+                return_z(g, t, part).start()
+            zin[g * 4 + z, :, columns] = ret[own_block(g, z), :, columns]
+
+    def return_y(g, part):
+        at = part_of(g, part)
+        return remote(
+            zsum.at[pl.ds(2 * g, 2), :, at], fin.at[pl.ds(2 * y, 2), :, at],
+            bs_sem.at[g * 2 + part], br_sem.at[g * 2 + part], device(behind[g], z, k),
         )
 
     home = pltpu.make_async_copy(zsum.at[pl.ds(0, 2)], fin.at[pl.ds(2 * y, 2)], fk_sem)
 
-    def relay_back(p):
+    def relay_back(p, part):
         for g in PASSES[p]:
             for t in range(3):
-                return_arrival(g, t).wait_recv()
-
-            def add(i, carry, g=g):
-                zsum[2 * g + i] = plus(zin[g * 4 + 2 * i], zin[g * 4 + 2 * i + 1])
+                return_arrival(g, t, part).wait_recv()
+            columns = part_of(g, part)
+
+            def add(i, carry, g=g, columns=columns):
+                zsum[2 * g + i, :, columns] = plus(
+                    zin[g * 4 + 2 * i, :, columns], zin[g * 4 + 2 * i + 1, :, columns]
+                )
                 return carry
 
             lax.fori_loop(0, 2, add, 0)
             if g == 0:
                 home.start()
             else:
-                return_y(g).start()
+                return_y(g, part).start()
 
     own.start()
     for t in range(3):
@@ -347,26 +391,27 @@
     along_z(3, 1).start()
     arrive(2, 1)
     along_z(3, 2).start()
-    back(0)
+    back(0, 0)
     arrive(2, 2)
     forward(2).start()
+    spread(0)
+    give_back(0, 0)
     exchanged(0)
+    arrive(3, 0)
+    arrive(3, 1)
+    arrive(3, 2)
+    forward(3).start()
+    exchanged(1)
     terms(1)
-    give_back(0)
-    back(1)
-    exchanged(1)
-    for t in range(3):
-        arrive(3, t)
-    forward(3).start()
-    give_back(1)
-    terms(2)
-    back(2)
-    give_back(2)
-    relay_back(0)
+    back(1, 0)
+    relay_back(0, 0)
+    give_back(1, 0)
+    back(1, 1)
+    give_back(1, 1)
     exchanged(2)
-    relay_back(1)
+    relay_back(1, 0)
     exchanged(3)
-    relay_back(2)
+    relay_back(1, 1)
 
     for g in range(4):
         for d in range(3):
@@ -374,22 +419,33 @@
     for p in range(len(PASSES)):
         keep(p).wait()
         keep_terms(p).wait()
-        for d in range(3):
-            gather(p, d).wait()
+        for side in (0, 1):
+            gather(p, side).wait_send()
+            if RELAYED[p]:
+                hand_on(p, side).wait()
+            else:
+                gather(p, side).wait_recv()
+        if not RELAYED[p]:
+            gather_far(p).wait()
     home.wait()
-    for g in range(1, 4):
-        return_y(g).wait()
-        for far in (0, 1):
-            along_y(g, far).wait_send()
+    for p in range(len(PASSES)):
+        for g in PASSES[p]:
+            for part in range(len(PARTS[p])):
+                to_sibling(g, part).wait_send()
+                for t in range(3):
+                    return_z(g, t, part).wait_send()
+                if g > 0:
+                    return_y(g, part).wait()
     for g in range(4):
+        if g > 0:
+            for far in (0, 1):
+                along_y(g, far).wait_send()
         for t in range(3):
             along_z(g, t).wait_send()
-            return_z(g, t).wait_send()
         for d in range(3):
             exchange(g, d).wait_send()
             exchange_forward(g, d).wait_send()
         forward(g).wait_send()
-        to_sibling(g).wait_send()
 
 
 def finish_kernel(xbuf, dall, fin, pick, gt, gg, gu, gd, hid_t):
@@ -454,8 +510,8 @@
             dma((8,)), dma((8,)), dma((12,)), dma((12,)),
             dma((groups,)), dma((groups,)),
             dma((12,)), dma((12,)), dma((12,)), dma((12,)),
-            dma((3 * passes,)), dma((3 * passes,)),
-            dma((groups,)), dma((groups,)), dma((12,)), dma((12,)), dma((groups,)), dma((groups,)),
+            dma((4 * passes,)), dma((4 * passes,)),
+            dma((8,)), dma((8,)), dma((24,)), dma((24,)), dma((8,)), dma((8,)),
         ],
         compiler_params=pltpu.CompilerParams(
             collective_id=0, has_side_effects=True, vmem_limit_bytes=44 * 1024 * 1024

time: 97.4 us -> 92.2 us (0.947)
  Pallas kernels: 95.8 us -> 90.6 us
    pallas_call x1, Pallas kernels: 87.9 us -> 82.7 us  [body(): pl.pallas_call(exchange_kernel, out_shape=(pltpu.VMEM((DP, BLOCKS, ROW, q...]
where the time goes in v4:
time: 92.2 us; the launch traced here: 91.9 us
  Pallas kernels  90.6 us (98%)
    pallas_call x1, Pallas kernels, body(): pl.pallas_call(exchange_kernel, out_shape=(pltpu.VMEM((DP, BLOCKS, ROW, q...  82.7 us
    pallas_call x1, Pallas kernels, body(): pl.pallas_call(finish_kernel, grid=(steps,), out_shape=(jax.ShapeDtypeStr...  7.88 us

profile of v4, /device:TPU:1, one launch (start us, length us, event | category | flops | bytes accessed | tf_op | source)
XLA Modules:
  0.0 91.9 jit_solution(11165938113900189554)
XLA Ops:
  0.6 82.7 %shard_map.102 = (bf16[4,32,16,1792]{3,2,1,0:T(8,128)(2,1)S(1)}, bf16[4,256,1152]{2,1,0:T(8,128)(2,1)S(1)}, bf16[8,16,3584]{2,1,0:T(8,128)(2,1)S(1)}, bf16[64,128]{1,0:T(8,128)(2,1)}) custom-call(bf16[128,7168]{1,0:T(8,128)(2,1)} %tokens.1, bf16[128,7168]{1,0:T(8,128)(2,1)} %grad_out.1, s32[8,128]{1,0:T(8,128)} %bitcast.2, f32[8,128]{1,0:T(8,128)} %bitcast.3, ...), custom_call_target="tpu_custom_call" | custom-call | flops 7046430720 | bytes 26000000 | tf_op jit(solution)/shard_map/pallas_call | solution.py:486
  83.3 0.0 copy-start
  83.3 0.7 copy-done
  84.0 7.9 %shard_map.103 = (bf16[128,7168]{1,0:T(8,128)(2,1)}, bf16[1792,384]{1,0:T(8,128)(2,1)}, bf16[1792,384]{1,0:T(8,128)(2,1)}, bf16[384,1792]{1,0:T(8,128)(2,1)}) custom-call(bf16[4,32,16,1792]{3,2,1,0:T(8,128)(2,1)S(1)} %get-tuple-element.8.xbuf, bf16[4,256,1152]{2,1,0:T(8,128)(2,1)S(1)} %get-tuple-element.9.dall, ...), custom_call_target="tpu_custom_call" | custom-call | flops 4227858432 | bytes 18000000 | tf_op jit(solution)/shard_map/pallas_call | solution.py:526
Async XLA Ops:
  83.3 0.7 copy-start

commit v5 on v4

--- a/solution.py
+++ b/solution.py
@@ -12,7 +12,7 @@
 BLOCKS = 32
 DY = (0, 1, 3, 2)
 PASSES = ((0, 1), (2, 3))
-KCH = 1024
+KCH = 1792
 NB = 512
 MESH = pl.DeviceIdType.MESH
 RELAYED = (True, False)
@@ -401,11 +401,11 @@
     arrive(3, 1)
     arrive(3, 2)
     forward(3).start()
+    terms(1)
     exchanged(1)
-    terms(1)
     back(1, 0)
+    give_back(1, 0)
     relay_back(0, 0)
-    give_back(1, 0)
     back(1, 1)
     give_back(1, 1)
     exchanged(2)

time: 92.2 us -> 91.8 us (level)
  no operation moved by 1% of the time
where the time goes in v5:
time: 91.8 us; the launch traced here: 91.5 us
  Pallas kernels  90.1 us (98%)
    pallas_call x1, Pallas kernels, body(): pl.pallas_call(exchange_kernel, out_shape=(pltpu.VMEM((DP, BLOCKS, ROW, q...  82.3 us
    pallas_call x1, Pallas kernels, body(): pl.pallas_call(finish_kernel, grid=(steps,), out_shape=(jax.ShapeDtypeStr...  7.89 us

profile of v5, /device:TPU:1, one launch (start us, length us, event | category | flops | bytes accessed | tf_op | source)
XLA Modules:
  0.0 91.5 jit_solution(6842814978998620816)
XLA Ops:
  0.6 82.3 %shard_map.102 = (bf16[4,32,16,1792]{3,2,1,0:T(8,128)(2,1)S(1)}, bf16[4,256,1152]{2,1,0:T(8,128)(2,1)S(1)}, bf16[8,16,3584]{2,1,0:T(8,128)(2,1)S(1)}, bf16[64,128]{1,0:T(8,128)(2,1)}) custom-call(bf16[128,7168]{1,0:T(8,128)(2,1)} %tokens.1, bf16[128,7168]{1,0:T(8,128)(2,1)} %grad_out.1, s32[8,128]{1,0:T(8,128)} %bitcast.2, f32[8,128]{1,0:T(8,128)} %bitcast.3, ...), custom_call_target="tpu_custom_call" | custom-call | flops 7046430720 | bytes 26000000 | tf_op jit(solution)/shard_map/pallas_call | solution.py:486
  82.9 0.0 copy-start
  82.9 0.7 copy-done
  83.6 7.9 %shard_map.103 = (bf16[128,7168]{1,0:T(8,128)(2,1)}, bf16[1792,384]{1,0:T(8,128)(2,1)}, bf16[1792,384]{1,0:T(8,128)(2,1)}, bf16[384,1792]{1,0:T(8,128)(2,1)}) custom-call(bf16[4,32,16,1792]{3,2,1,0:T(8,128)(2,1)S(1)} %get-tuple-element.8.xbuf, bf16[4,256,1152]{2,1,0:T(8,128)(2,1)S(1)} %get-tuple-element.9.dall, ...), custom_call_target="tpu_custom_call" | custom-call | flops 4227858432 | bytes 18000000 | tf_op jit(solution)/shard_map/pallas_call | solution.py:526
Async XLA Ops:
  82.9 0.7 copy-start
